TPU v7x, 256 devices: a whole 4x4x8 slice. The times are simulated.
256 devices in a mesh: dp: 8 (over y, core), proto: 32 (over z, x).
Axes of the slice: x: 4, y: 4, z: 8, core: 2. Of those that a mesh axis runs over, the one named last changes fastest.
Arguments:
- embeddings: bfloat16 [8192, 256], P('dp'), may hold values from -0.375 to 0.375
- queue: bfloat16 [8192, 256], P('dp'), may hold values from -0.375 to 0.375
- prototypes: bfloat16 [256, 65536], P(None, 'proto'), may hold values from -0.375 to 0.375
- pairing: int32 [8192], P('dp'), may hold values from 0 to 8191, as said below
Outputs:
- grad_embed: float32 [8192, 256], P('dp')
- grad_proto: float32 [256, 65536], P(None, 'proto')
- loss_mean: float32 [], replicated
Inputs may be any that keep to these rules, and one draw needn't show every extreme that they name: pairing[pairing[i]] = i and pairing[i] != i; i and pairing[i] lie in the same aligned block of 1024 rows.
All inputs are finite; a program needn't handle non-finite values.
Results may differ from a plain program's by a relative error of at most 0.0011.
The roundings to bfloat16 on the way count: a program that leaves them out, or rounds other values in their place, can miss the bound.
Values sent between devices are 32-bit elements; how exact they have to be, the bound alone decides.
A program may use at most 128 MiB of HBM per device.

v0:
```python
import math

import jax
import jax.numpy as jnp
from jax import lax
from jax.sharding import PartitionSpec as P

PROTOS = 65536
ITERS = 3


EPS_SINK = 0.05
TEMPER = 0.1
HIGHEST_PREC = lax.Precision.HIGHEST


def unit_rows(values):
    return values * lax.rsqrt(jnp.sum(values * values, axis=1, keepdims=True) + 1e-06)


def unit_cols(values):
    return values * lax.rsqrt(jnp.sum(values * values, axis=0, keepdims=True) + 1e-06)


def local(embeddings, queue, prototypes, pairing):
    dp_count = lax.axis_size("dp")
    crop_rows = embeddings.shape[0]
    total_rows = (crop_rows + queue.shape[0]) * dp_count
    total_crops = crop_rows * dp_count
    embed_unit, embed_back = jax.vjp(unit_rows, embeddings.astype(jnp.float32))
    proto_unit, proto_back = jax.vjp(unit_cols, prototypes.astype(jnp.float32))
    embed_bf = embed_unit.astype(jnp.bfloat16)
    queue_bf = unit_rows(queue.astype(jnp.float32)).astype(jnp.bfloat16)
    proto_bf = proto_unit.astype(jnp.bfloat16)
    all_rows = jnp.concatenate([embed_bf, queue_bf], axis=0)
    scores = jnp.dot(all_rows, proto_bf, preferred_element_type=jnp.float32)
    exponent = jnp.exp(scores / EPS_SINK)
    row_scale = jnp.ones((all_rows.shape[0],), jnp.float32)
    col_scale = jnp.ones((proto_bf.shape[1],), jnp.float32)
    for sweep_index in range(ITERS):
        col_sum = lax.psum(jnp.dot(row_scale, exponent, precision=HIGHEST_PREC), "dp")
        col_scale = 1.0 / (PROTOS * col_sum)
        partial_rows = jnp.dot(exponent, col_scale, precision=HIGHEST_PREC)
        row_scale = 1.0 / (total_rows * lax.psum(partial_rows, "proto"))
    local_pair = pairing - lax.axis_index("dp") * crop_rows
    partner_scale = jnp.take(row_scale[:crop_rows] * total_rows, local_pair)
    partner_exp = jnp.take(exponent[:crop_rows], local_pair, axis=0)
    codes = partner_exp * col_scale[None, :] * partner_scale[:, None]
    scores_crop = scores[:crop_rows]
    soft_exp = jnp.exp(scores_crop / TEMPER)
    soft_total, code_score = lax.psum(
        (jnp.sum(soft_exp, axis=1), jnp.sum(codes * scores_crop, axis=1) / TEMPER), "proto"
    )
    cross_ent = jnp.log(soft_total) - code_score
    loss_mean = lax.psum(jnp.sum(cross_ent), "dp") / total_crops
    differ = ((soft_exp / soft_total[:, None] - codes) / TEMPER).astype(jnp.bfloat16)
    embed_factor = math.sqrt(PROTOS)
    embed_cot = lax.psum(
        lax.dot_general(
            differ, proto_bf, (((1,), (1,)), ((), ())), preferred_element_type=jnp.float32
        ),
        "proto",
    )
    grad_embed = embed_factor * embed_back(embed_cot)[0]
    proto_factor = PROTOS / math.sqrt(total_crops)
    proto_cot = lax.psum(
        lax.dot_general(
            embed_bf, differ, (((0,), (0,)), ((), ())), preferred_element_type=jnp.float32
        ),
        "dp",
    )
    grad_proto = proto_factor * proto_back(proto_cot)[0]
    return (grad_embed, grad_proto, loss_mean)


def solution(mesh):
    return jax.shard_map(
        local,
        mesh=mesh,
        in_specs=(P("dp", None), P("dp", None), P(None, "proto"), P("dp")),
        out_specs=(P("dp", None), P(None, "proto"), P()),
        check_vma=False,
    )
```

profile of v0, /device:TPU:2, one launch (start us, length us, event | category | flops | bytes accessed | tf_op | source)
XLA Modules:
  0.0 747.1 jit_solution(4036557978979942669)
XLA Ops:
  7.2 0.0 all-reduce.4.cloned.1.call-start
  7.2 1.5 fusion.2
  8.7 1.3 fusion.5
  10.0 1.3 fusion.8
  11.2 1.5 fusion.6
  12.8 14.0 %multiply_exponential_fusion = (f32[2048,2048]{0,1:T(8,128)}, f32[2048,2048]{0,1:T(8,128)}) fusion(bf16[256,2048]{1,0:T(8,128)(2,1)} %param.6, f32[2048]{0:T(1024)S(1)} %add_rsqrt_fusion, bf16[1024,256]{1,0:T(8,128)(2,1)S(1)} %get-tuple-element.11, bf16[1024,256]{1,0:T(8,128)(2,1)S(1)} %get-tuple-element.12), kind=kOutput, calls=%fused_computation.2 | convolution fusion | flops 2155347968 | bytes 35659776 | tf_op jit(solution)/shard_map/dot_general | solution.py:36
  26.7 8.2 %slice.17 = f32[1024,2048]{0,1:T(8,128)} slice(f32[2048,2048]{0,1:T(8,128)} %get-tuple-element.9), slice={[0:1024], [0:2048]} | slice | bytes 16777216 | tf_op jit(solution)/shard_map/slice | solution.py:47
  35.0 0.0 copy-start.3
  35.0 9.2 %copy.9 = f32[1024,2048]{1,0:T(8,128)} copy(f32[1024,2048]{0,1:T(8,128)} %slice.17) | data formatting | bytes 16777216 | tf_op jit(solution)/shard_map/slice | solution.py:47
  44.1 0.0 copy-done.3
  44.1 12.5 %gather_fusion = f32[1024,2048]{1,0:T(8,128)} fusion(f32[1024,2048]{1,0:T(8,128)} %copy.9, s32[1024]{0:T(1024)S(1)} %fusion.22), kind=kCustom, calls=%fused_computation | custom fusion | bytes 16781312 | tf_op jit(solution)/shard_map/jit(_take)/gather | solution.py:47
  56.6 9.3 %copy.10 = f32[1024,2048]{0,1:T(8,128)} copy(f32[1024,2048]{1,0:T(8,128)} %gather_fusion) | data formatting | bytes 16777216 | tf_op jit(solution)/shard_map/jit(_take)/gather | solution.py:47
  65.9 17.4 %fusion.20 = f32[1,2048]{1,0:T(1,128)S(1)} fusion(f32[2048,2048]{0,1:T(8,128)} %get-tuple-element.10), kind=kOutput, calls=%fused_computation.46 | convolution fusion | flops 54525952 | bytes 16785408 | tf_op jit(solution)/shard_map/dot_general | solution.py:41
  83.3 15.3 %psum.78 = f32[2048]{0:T(1024)S(1)} all-reduce(f32[2048]{0:T(1024)S(1)} %bitcast.29), channel_id=1, replica_groups=mesh['dp'=8,'proto'=32] {'dp'}, use_global_device_ids=true, to_apply=%region_5.0 | all-reduce | flops 2048 | bytes 16384 | tf_op jit(solution)/shard_map/psum | solution.py:41
  98.6 13.7 %fusion.29 = f32[1,2048]{1,0:T(1,128)S(1)} fusion(f32[2048,1]{0,1:T(1,128)S(1)} %bitcast.27, f32[2048,2048]{0,1:T(8,128)} %get-tuple-element.10), kind=kOutput, calls=%fused_computation.62 | convolution fusion | flops 54525952 | bytes 16793600 | tf_op jit(solution)/shard_map/dot_general | solution.py:43
  112.3 74.8 %psum.79 = f32[2048]{0:T(1024)S(1)} all-reduce(f32[2048]{0:T(1024)S(1)} %bitcast.20), channel_id=1, replica_groups=mesh['dp'=8,'proto'=32] {'proto'}, use_global_device_ids=true, to_apply=%region_6.0 | all-reduce | flops 2048 | bytes 16384 | tf_op jit(solution)/shard_map/psum | solution.py:44
  187.1 17.5 %fusion.28 = f32[1,2048]{1,0:T(1,128)S(1)} fusion(f32[2048,1]{0,1:T(1,128)S(1)} %bitcast.23, f32[2048,2048]{0,1:T(8,128)} %get-tuple-element.10), kind=kOutput, calls=%fused_computation.61 | convolution fusion | flops 54525952 | bytes 16793600 | tf_op jit(solution)/shard_map/dot_general | solution.py:41
  204.6 12.9 %psum.80 = f32[2048]{0:T(1024)S(1)} all-reduce(f32[2048]{0:T(1024)S(1)} %bitcast.24), channel_id=1, replica_groups=mesh['dp'=8,'proto'=32] {'dp'}, use_global_device_ids=true, to_apply=%region_7.0 | all-reduce | flops 2048 | bytes 16384 | tf_op jit(solution)/shard_map/psum | solution.py:41
  217.5 13.7 %fusion.27 = f32[1,2048]{1,0:T(1,128)S(1)} fusion(f32[2048,1]{0,1:T(1,128)S(1)} %bitcast.28, f32[2048,2048]{0,1:T(8,128)} %get-tuple-element.10), kind=kOutput, calls=%fused_computation.60 | convolution fusion | flops 54525952 | bytes 16793600 | tf_op jit(solution)/shard_map/dot_general | solution.py:43
  231.2 75.1 %psum.81 = f32[2048]{0:T(1024)S(1)} all-reduce(f32[2048]{0:T(1024)S(1)} %bitcast.21), channel_id=1, replica_groups=mesh['dp'=8,'proto'=32] {'proto'}, use_global_device_ids=true, to_apply=%region_8.0 | all-reduce | flops 2048 | bytes 16384 | tf_op jit(solution)/shard_map/psum | solution.py:44
  306.3 17.5 %fusion.26 = f32[1,2048]{1,0:T(1,128)S(1)} fusion(f32[2048,1]{0,1:T(1,128)S(1)} %bitcast.25, f32[2048,2048]{0,1:T(8,128)} %get-tuple-element.10), kind=kOutput, calls=%fused_computation.59 | convolution fusion | flops 54525952 | bytes 16793600 | tf_op jit(solution)/shard_map/dot_general | solution.py:41
  323.8 12.9 %psum.82 = f32[2048]{0:T(1024)S(1)} all-reduce(f32[2048]{0:T(1024)S(1)} %bitcast.26), channel_id=1, replica_groups=mesh['dp'=8,'proto'=32] {'dp'}, use_global_device_ids=true, to_apply=%region_9.10 | all-reduce | flops 2048 | bytes 16384 | tf_op jit(solution)/shard_map/psum | solution.py:41
  336.7 13.7 %fusion.25 = f32[1,2048]{1,0:T(1,128)S(1)} fusion(f32[2048,1]{0,1:T(1,128)S(1)} %bitcast.19, f32[2048,2048]{0,1:T(8,128)} %get-tuple-element.10), kind=kOutput, calls=%fused_computation.58 | convolution fusion | flops 54525952 | bytes 16793600 | tf_op jit(solution)/shard_map/dot_general | solution.py:43
  350.4 70.6 %psum.83 = f32[2048]{0:T(1024)S(1)} all-reduce(f32[2048]{0:T(1024)S(1)} %bitcast.22), channel_id=1, replica_groups=mesh['dp'=8,'proto'=32] {'proto'}, use_global_device_ids=true, to_apply=%region_10.11 | all-reduce | flops 2048 | bytes 16384 | tf_op jit(solution)/shard_map/psum | solution.py:44
  421.1 4.5 gather_fusion.1
  425.6 7.1 multiply_reduce_fusion
  432.8 72.7 %all-reduce = (f32[1024]{0:T(1024)S(1)}, f32[1024]{0:T(1024)S(1)}) all-reduce(f32[1024]{0:T(1024)S(1)} %get-tuple-element.4, f32[1024]{0:T(1024)S(1)} %broadcast_multiply_fusion), channel_id=1, replica_groups=mesh['dp'=8,'proto'=32] {'proto'}, use_global_device_ids=true, to_apply=%region_4.0 | all-reduce | flops 2048 | bytes 16384 | tf_op jit(solution)/shard_map/psum | solution.py:51
  505.4 0.0 copy-start
  505.4 7.3 multiply_convert_fusion
  512.7 0.0 copy-start.2
  512.7 1.9 copy-done.2
  514.6 0.0 copy-done
  514.6 0.0 copy-start.1
  514.7 2.3 fusion.15
  517.0 0.0 all-reduce.4.cloned.1.call-update
  517.0 0.0 all-reduce.6.cloned.1.call-start
  517.0 4.8 fusion.30
  521.9 0.0 all-reduce.6.cloned.1.call-update
  521.9 0.6 subtract_reduce_fusion
  522.5 13.1 %psum.87 = f32[]{:T(128)} all-reduce(f32[]{:T(128)} %subtract_reduce_fusion), channel_id=1, replica_groups=mesh['dp'=8,'proto'=32] {'dp'}, use_global_device_ids=true, to_apply=%region_18.19 | all-reduce | flops 1 | bytes 8 | tf_op jit(solution)/shard_map/psum | solution.py:55
  536.3 122.2 %all-reduce.4.cloned.1.call-done = f32[1024,256]{1,0:T(8,128)} async-done(((f32[1024,256]{1,0:T(8,128)}), f32[1024,256]{1,0:T(8,128)}) %all-reduce.4.cloned.1.call-update) | async-done | bytes 1048592 | tf_op jit(solution)/shard_map/psum | solution.py:58
  658.5 0.0 copy-done.1
  658.5 1.4 fusion.10
  659.9 71.0 %all-reduce.6.cloned.1.call-done = f32[256,2048]{1,0:T(8,128)} async-done(((f32[256,2048]{1,0:T(8,128)}), f32[256,2048]{1,0:T(8,128)}) %all-reduce.6.cloned.1.call-update) | async-done | bytes 2097168 | tf_op jit(solution)/shard_map/psum | solution.py:66
  730.9 1.9 fusion.4
  732.8 2.5 fusion.7
  735.3 3.3 fusion.1
  (14 shorter events, 0.1 us)
Async XLA Ops:
  7.2 651.3 %all-reduce.4.cloned.1.call-start = ((), (), s32[]{:S(2)}) async-start(), calls=%async_computation | async-start | bytes 2097152 | tf_op jit(solution)/shard_map/psum | solution.py:58
  35.0 9.2 %copy-start.3 = (s32[1024]{0:T(1024)S(1)}, s32[1024]{0:T(1024)}, u32[]{:S(2)}) copy-start(s32[1024]{0:T(1024)} %param.7) | copy-start | bytes 12292
  505.4 9.2 %copy-start = (bf16[256,2048]{1,0:T(8,128)(2,1)S(1)}, bf16[256,2048]{1,0:T(8,128)(2,1)}, u32[]{:S(2)}) copy-start(bf16[256,2048]{1,0:T(8,128)(2,1)} %param.6) | copy-start | bytes 3145732
  512.7 1.9 copy-start.2
  514.6 143.8 %copy-start.1 = (bf16[1024,256]{1,0:T(8,128)(2,1)S(1)}, bf16[1024,256]{1,0:T(8,128)(2,1)}, u32[]{:S(2)}) copy-start(bf16[1024,256]{1,0:T(8,128)(2,1)} %param.4) | copy-start | bytes 1572868
  517.0 213.9 %all-reduce.6.cloned.1.call-start = ((), (), s32[]{:S(2)}) async-start(), calls=%async_computation.1 | async-start | bytes 4194304 | tf_op jit(solution)/shard_map/psum | solution.py:66
Sparse Core Ops, SparseCore 0:
  517.1 141.2 all-reduce.3
  661.4 69.4 all-reduce.5
where the time goes:
time: 756 us; the launch traced here: 747 us
  blocking collectives  347 us (46%)
  waiting for transfers between devices  193 us (26%)
  matrix products  115 us (15%)
  local copies, waits for them, and re-layouts  45.6 us (6%)
  other arithmetic  29.8 us (4%)
  between operations  16.5 us (2%)
    psum x3, blocking collectives, local(): row_scale = 1.0 / (total_rows * lax.psum(partial_rows, 'proto'))  220 us
    psum x1, waiting for transfers between devices, local(): lax.psum(lax.dot_general(differ, proto_bf, (((1,), (1,)), ((), ())), pref...  122 us
    psum x1, blocking collectives, local(): lax.psum((jnp.sum(soft_exp, axis=1), jnp.sum(codes * scores_crop, axis=1)...  72.7 us
    psum x1, waiting for transfers between devices, local(): lax.psum(lax.dot_general(embed_bf, differ, (((0,), (0,)), ((), ())), pref...  71 us
    dot_general x3, matrix products, local(): jnp.dot(row_scale, exponent, precision=HIGHEST_PREC)  52.3 us
    dot_general x3, matrix products, local(): partial_rows = jnp.dot(exponent, col_scale, precision=HIGHEST_PREC)  41.2 us
    psum x3, blocking collectives, local(): lax.psum(jnp.dot(row_scale, exponent, precision=HIGHEST_PREC), 'dp')  41.1 us
    gather x2, local copies, waits for them, and re-layouts, local(): partner_exp = jnp.take(exponent[:crop_rows], local_pair, axis=0)  21.7 us
  transfers between devices with their start and end apart: 2, of which 2 were waited for; matrix products, arithmetic and copies ran while one was open for 1% of the time, Pallas kernels for 0%

commit v1 on v0

v1 whole, which is shorter than its diff:
```python
import functools
import math

import jax
import jax.numpy as jnp
from jax import lax
from jax.experimental import pallas as pl
from jax.experimental.pallas import tpu as pltpu
from jax.sharding import PartitionSpec as P

PROTOS = 65536
ITERS = 3
CORES = 2
ALONG_X = 4
LOG2E = math.log2(math.e)
F32 = jnp.float32
BF16 = jnp.bfloat16
MESH = pl.DeviceIdType.MESH


def inv_norm(sum_sq):
    shifted = sum_sq + 1e-06
    guess = lax.rsqrt(shifted)
    return guess * (1.5 - 0.5 * shifted * guess * guess)


def aligned(index, size):
    return pl.ds(pl.multiple_of(index * size, size), size)


class Exchange:
    def __init__(self, buf, send_sem, recv_sem, me, size, device):
        self.buf, self.me, self.size, self.device = buf, me, size, device
        self.send_sem, self.recv_sem = send_sem, recv_sem

    def copy(self, hop, slot):
        return pltpu.make_async_remote_copy(
            src_ref=self.buf.at[self.me],
            dst_ref=self.buf.at[slot],
            send_sem=self.send_sem.at[hop],
            recv_sem=self.recv_sem.at[slot],
            device_id=self.device(lax.rem(self.me + hop, self.size)),
            device_id_type=MESH,
        )

    def start(self, block):
        self.buf[self.me] = block
        for hop in range(1, self.size):
            self.copy(hop, self.me).start()

    def finish(self):
        for hop in range(1, self.size):
            self.copy(hop, lax.rem(self.me + hop, self.size)).wait_recv()
        for hop in range(1, self.size):
            self.copy(hop, self.me).wait_send()
        total = self.buf[0]
        for slot in range(1, self.size):
            total = total + self.buf[slot]
        return total


class Ring:
    def __init__(self, n, me, part, recv, send_sem, recv_sem, device):
        self.n, self.me, self.part, self.recv = n, me, part, recv
        self.send_sem, self.recv_sem, self.device = send_sem, recv_sem, device
        self.far = n // 2
        self.sent = []

    def at(self, hops):
        return lax.rem(self.me + hops + self.n, self.n)

    def copy(self, way, step, half, piece):
        return pltpu.make_async_remote_copy(
            src_ref=self.part(piece, half),
            dst_ref=self.recv.at[way, step - 1, half],
            send_sem=self.send_sem.at[way, step - 1, half],
            recv_sem=self.recv_sem.at[way, step - 1, half],
            device_id=self.device(self.at(1 if way == 0 else -1)),
            device_id_type=MESH,
        )

    def send(self, way, step, half, piece):
        copy = self.copy(way, step, half, piece)
        copy.start()
        self.sent.append(copy)

    def take(self, way, step, half, piece):
        self.copy(way, step, half, piece).wait_recv()
        view = self.part(piece, half)
        view[...] = view[...] + self.recv[way, step - 1, half]

    def target(self, way, step):
        hops = self.far - step + 1
        return self.at(hops if way == 0 else -hops)

    def first(self):
        if self.n > 1:
            for way in range(2):
                self.send(way, 1, way, self.at(self.far))

    def early(self, way):
        if self.far >= 2:
            self.send(way, 2, 1 - way, self.target(way, 2))

    def second(self):
        if self.far >= 2:
            for way in range(2):
                piece = self.target(way, 2)
                self.take(way, 1, way, piece)
                self.send(way, 2, way, piece)

    def step(self, step):
        if 2 < step <= self.far:
            for way in range(2):
                piece = self.target(way, step)
                for half in (way, 1 - way):
                    self.take(way, step - 1, half, piece)
                    self.send(way, step, half, piece)

    def finish(self):
        if self.n == 2:
            for way in range(2):
                self.take(way, 1, way, self.me)
        elif self.n > 2:
            for way in range(2):
                for half in range(2):
                    self.take(way, self.far, half, self.me)

    def close(self):
        for copy in self.sent:
            copy.wait_send()


class Gather:
    def __init__(self, n, me, view, send_sem, recv_sem, device):
        self.n, self.me, self.view = n, me, view
        self.send_sem, self.recv_sem, self.device = send_sem, recv_sem, device
        self.far = n // 2
        self.sent = []

    def at(self, hops):
        return lax.rem(self.me + hops + self.n, self.n)

    def halves(self, way, hops):
        return (way, 1 - way) if hops < self.far else (way,)

    def copy(self, way, hops, half, piece):
        return pltpu.make_async_remote_copy(
            src_ref=self.view(piece, half),
            dst_ref=self.view(piece, half),
            send_sem=self.send_sem.at[way, hops - 1, half],
            recv_sem=self.recv_sem.at[way, hops - 1, half],
            device_id=self.device(self.at(1 if way == 0 else -1)),
            device_id_type=MESH,
        )

    def source(self, way, hops):
        return self.at(-hops if way == 0 else hops)

    def forward(self, way, hops):
        if hops <= self.far:
            piece = self.source(way, hops - 1)
            for half in self.halves(way, hops):
                copy = self.copy(way, hops, half, piece)
                copy.start()
                self.sent.append(copy)

    def first(self):
        if self.n > 1:
            for way in range(2):
                self.forward(way, 1)

    def take(self, way, hops):
        if 1 <= hops <= self.far:
            piece = self.source(way, hops)
            for half in self.halves(way, hops):
                self.copy(way, hops, half, piece).wait_recv()
                if hops < self.far and half in self.halves(way, hops + 1):
                    copy = self.copy(way, hops + 1, half, piece)
                    copy.start()
                    self.sent.append(copy)

    def rest(self):
        for hops in range(1, self.far + 1):
            for way in range(2):
                self.take(way, hops)

    def close(self):
        for copy in self.sent:
            copy.wait_send()


def kernel(
    sizes,
    emb,
    que,
    pro,
    pair,
    out_e,
    out_p,
    out_l,
    ex,
    sx,
    yx,
    rows_bf,
    part_bf,
    pro_bf,
    emb_t,
    pro_t,
    differ,
    colacc,
    lanes,
    softp,
    rbc,
    stb,
    qpart,
    dpbuf,
    xbuf,
    zbuf,
    ldp,
    lx,
    lz,
    pc,
    sib,
    yrecv,
    ag,
    h1,
    h2,
    x1recv,
    z1recv,
    z2recv,
    x2recv,
    e1,
    e2,
    dp_sems,
    x_sems,
    z_sems,
    ldp_sems,
    lx_sems,
    lz_sems,
    sib_sems,
    y_sems,
    x1_sems,
    z1_sems,
    z2_sems,
    x2_sems,
    yg_sems,
    sg_sems,
    z1g_sems,
    x1g_sems,
    x2g_sems,
    z2g_sems,
    op_sems,
    oe_sems,
):
    ny, nx, nz = sizes
    dp_count = ny * CORES
    crops, depth = emb.shape
    rows = crops + que.shape[0]
    cols = pro.shape[1]
    total_rows = rows * dp_count
    total_crops = crops * dp_count
    lane_blocks = cols // 128
    row_blocks = rows // 128
    crop_blocks = crops // 128
    width = cols // dp_count
    tile = 256

    my_dp = lax.axis_index("dp")
    my_proto = lax.axis_index("proto")
    my_y, my_c = my_dp // CORES, lax.rem(my_dp, CORES)
    my_z, my_x = my_proto // nx, lax.rem(my_proto, nx)

    def on_dp(index):
        return (index, my_proto)

    def on_x(index):
        return (my_dp, my_z * nx + index)

    def on_z(index):
        return (my_dp, index * nx + my_x)

    def on_y(index):
        return (index * CORES + my_c, my_proto)

    sibling = (my_y * CORES + 1 - my_c, my_proto)

    barrier = pltpu.get_barrier_semaphore()
    for me, size, device in ((my_dp, dp_count, on_dp), (my_x, nx, on_x), (my_z, nz, on_z)):
        for hop in range(1, size):
            pl.semaphore_signal(
                barrier, inc=1, device_id=device(lax.rem(me + hop, size)), device_id_type=MESH
            )

    @pl.loop(0, crops // tile)
    def _(i):
        block = aligned(i, tile)
        for source, first in ((emb, 0), (que, crops)):
            values = source[block, :].astype(F32)
            inv = inv_norm(jnp.sum(values * values, axis=1, keepdims=True))
            start = pl.multiple_of(first + i * tile, tile)
            rows_bf[pl.ds(start, tile), :] = (values * inv).astype(BF16)

    @pl.loop(0, cols // tile)
    def _(j):
        block = aligned(j, tile)
        values = pro[:, block].astype(F32)
        inv = inv_norm(jnp.sum(values * values, axis=0, keepdims=True))
        pro_bf[:, block] = (values * inv).astype(BF16)

    softp[...] = jnp.zeros_like(softp)

    @pl.loop(0, cols // tile)
    def _(j):
        block = aligned(j, tile)
        weights = pro_bf[:, block]
        acc = jnp.zeros((8, tile), F32)
        for i in range(rows // tile):
            lines = slice(i * tile, (i + 1) * tile)
            scores = jnp.dot(rows_bf[lines, :], weights, preferred_element_type=F32)
            if i < crops // tile:
                sx[lines, block] = scores
                soft = jnp.exp2(scores * (10.0 * LOG2E))
                folded = soft[:, :128]
                for k in range(1, tile // 128):
                    folded = folded + soft[:, k * 128 : (k + 1) * 128]
                softp[lines, :] += folded
                expo = soft * soft
            else:
                expo = jnp.exp2(scores * (20.0 * LOG2E))
            ex[lines, block] = expo
            acc = acc + jnp.sum(expo.reshape(tile // 8, 8, tile), axis=0)
        colacc[j] = acc

    def dense_cols():
        pieces = []
        for j in range(lane_blocks):
            k, part = j * 128 // tile, (j * 128) % tile
            pieces.append(jnp.sum(colacc[k, :, part : part + 128], axis=0, keepdims=True))
        return jnp.concatenate(pieces, axis=0)

    def dense_rows(source, blocks):
        pieces = []
        for b in range(blocks):
            pieces.append(
                jnp.sum(source[b * 128 : (b + 1) * 128, :].T, axis=0, keepdims=True)
            )
        return jnp.concatenate(pieces, axis=0)

    def spread_rows(target, dense, blocks):
        for b in range(blocks):
            target[b * 128 : (b + 1) * 128, :] = jnp.broadcast_to(
                dense[b : b + 1, :], (128, 128)
            ).T

    def col_pass():
        groups = 4

        def step(i, accs):
            accs = list(accs)
            for g in range(groups):
                lines = pl.ds(pl.multiple_of(i * 8 * groups + 8 * g, 8), 8)
                scale = rbc[lines, :]
                for j in range(lane_blocks):
                    accs[j] = accs[j] + ex[lines, j * 128 : (j + 1) * 128] * scale
            return tuple(accs)

        accs = lax.fori_loop(
            0, rows // (8 * groups), step, (jnp.zeros((8, 128), F32),) * lane_blocks
        )
        return jnp.concatenate([jnp.sum(a, axis=0, keepdims=True) for a in accs], axis=0)

    def spread_cols(dense):
        return [
            jnp.broadcast_to(dense[j : j + 1, :], (8, 128)) for j in range(lane_blocks)
        ]

    def row_pass(scales):
        groups = 4

        @pl.loop(0, rows // (8 * groups))
        def _(i):
            for g in range(groups):
                lines = pl.ds(pl.multiple_of(i * 8 * groups + 8 * g, 8), 8)
                acc = ex[lines, :128] * scales[0]
                for j in range(1, lane_blocks):
                    acc = acc + ex[lines, j * 128 : (j + 1) * 128] * scales[j]
                lanes[lines, :] = acc

    def partner_pass(scales):
        groups = 4

        @pl.loop(0, crops // (8 * groups))
        def _(i):
            for g in range(groups):
                lines = pl.ds(pl.multiple_of(i * 8 * groups + 8 * g, 8), 8)
                acc = jnp.zeros((8, 128), F32)
                for j in range(lane_blocks):
                    block = slice(j * 128, (j + 1) * 128)
                    code = yx[lines, block] * scales[j]
                    yx[lines, block] = code
                    acc = acc + code
                lanes[lines, :] = acc

    def soften(first, last):
        groups = 2

        @pl.loop(first // (8 * groups), last // (8 * groups))
        def _(i):
            for g in range(groups):
                lines = pl.ds(pl.multiple_of(i * 8 * groups + 8 * g, 8), 8)
                scale = stb[lines, :]
                acc = jnp.zeros((8, 128), F32)
                for j in range(lane_blocks):
                    block = slice(j * 128, (j + 1) * 128)
                    score = sx[lines, block]
                    acc = acc + yx[lines, block] * score
                    sx[lines, block] = jnp.exp2(score * (10.0 * LOG2E)) * scale
                qpart[lines, :] = acc

    def partners():
        local_pair = pair[...] - my_dp * crops

        @pl.loop(0, crops // tile)
        def _(i):
            block = aligned(i, tile)
            line = lax.broadcasted_iota(jnp.int32, (tile, crops), 0) + i * tile
            pick = jnp.where(line == local_pair, 1.0, 0.0).astype(BF16)
            part_bf[block, :] = jnp.dot(
                pick, rows_bf[:crops, :], preferred_element_type=F32
            ).astype(BF16)

        @pl.loop(0, cols // tile)
        def _(j):
            block = aligned(j, tile)
            weights = pro_bf[:, block]
            for i in range(crops // tile):
                lines = slice(i * tile, (i + 1) * tile)
                scores = jnp.dot(part_bf[lines, :], weights, preferred_element_type=F32)
                soft = jnp.exp2(scores * (10.0 * LOG2E))
                yx[lines, block] = soft * soft

    def transposed_rows():
        @pl.loop(0, crops // tile)
        def _(i):
            block = aligned(i, tile)
            emb_t[:, block] = rows_bf[block, :].astype(F32).T.astype(BF16)

    def transposed_cols():
        @pl.loop(0, cols // tile)
        def _(j):
            block = aligned(j, tile)
            pro_t[block, :] = pro_bf[:, block].astype(F32).T.astype(BF16)

    pl.semaphore_wait(barrier, dp_count - 1 + nx - 1 + nz - 1)
    col_dense = dense_cols()
    soft_total = None
    row_sum = None
    for it in range(ITERS):
        over_dp = Exchange(
            dpbuf.at[it], dp_sems.at[it, 0], dp_sems.at[it, 1], my_dp, dp_count, on_dp
        )
        over_x = Exchange(
            xbuf.at[it], x_sems.at[it, 0], x_sems.at[it, 1], my_x, nx, on_x
        )
        over_z = Exchange(
            zbuf.at[it], z_sems.at[it, 0], z_sems.at[it, 1], my_z, nz, on_z
        )
        over_dp.start(col_dense)
        if it == 0:
            partners()
        elif it == 1:
            spread_rows(stb, 10.0 / soft_total, crop_blocks)
        elif it == 2:
            transposed_cols()
        col_scale = 1.0 / (PROTOS * over_dp.finish())
        blank = jnp.zeros((crop_blocks, 128), F32)
        if it < ITERS - 1:
            row_pass(spread_cols(col_scale))
            extra = dense_rows(softp, crop_blocks) if it == 0 else blank
            block = jnp.concatenate([dense_rows(lanes, row_blocks), extra], axis=0)
            over_x.start(block)
            if it == 0:
                transposed_rows()
            over_z.start(over_x.finish())
            total = over_z.finish()
            if it == 0:
                soft_total = total[row_blocks:, :]
            spread_rows(rbc, 1.0 / (total_rows * total[:row_blocks, :]), row_blocks)
            col_dense = col_pass()
        else:
            partner_pass(spread_cols(10.0 * col_scale))
            filler = jnp.zeros((row_blocks, 128), F32)
            over_x.start(
                jnp.concatenate([dense_rows(lanes, crop_blocks), filler], axis=0)
            )
            soften(0, crops // 2)
            over_z.start(over_x.finish())
            soften(crops // 2, crops)
            row_sum = over_z.finish()[:crop_blocks, :]

    spread_rows(rbc, 10.0 / row_sum, crop_blocks)

    def add_up(i, acc):
        lines = aligned(i, 8)
        return acc + qpart[lines, :] * rbc[lines, :]

    code_score = lax.fori_loop(0, crops // 8, add_up, jnp.zeros((8, 128), F32))
    log_total = jnp.log(soft_total) * (1.0 / (nx * nz))
    if crop_blocks != 8:
        log_total = jnp.broadcast_to(jnp.sum(log_total, axis=0, keepdims=True), (8, 128)) / 8.0
    loss_dp = Exchange(ldp, ldp_sems.at[0], ldp_sems.at[1], my_dp, dp_count, on_dp)
    loss_x = Exchange(lx, lx_sems.at[0], lx_sems.at[1], my_x, nx, on_x)
    loss_z = Exchange(lz, lz_sems.at[0], lz_sems.at[1], my_z, nz, on_z)
    loss_dp.start(log_total - code_score)

    def piece(t, core):
        block = aligned(t * CORES + core, width)
        for i in range(crops // tile):
            lines = slice(i * tile, (i + 1) * tile)
            scale = rbc[lines, :]
            scale = jnp.concatenate([scale] * (width // 128), axis=1)
            value = sx[lines, block] - yx[lines, block] * scale
            differ[lines, block] = value.astype(BF16)
        cot = jnp.dot(emb_t[...], differ[:, block], preferred_element_type=F32)
        half = depth // 2
        pc[t, core, 0] = cot[:half, :]
        pc[t, core, 1] = cot[half:, :]

    def to_sibling(order, t):
        return pltpu.make_async_remote_copy(
            src_ref=pc.at[t, 1 - my_c],
            dst_ref=sib.at[order],
            send_sem=sib_sems.at[0, order],
            recv_sem=sib_sems.at[1, order],
            device_id=sibling,
            device_id_type=MESH,
        )

    y_ring = Ring(
        ny,
        my_y,
        lambda t, half: pc.at[t, my_c, half],
        yrecv,
        y_sems.at[0],
        y_sems.at[1],
        on_y,
    )
    near = [] if ny < 4 else [1, -1]
    order = ([ny // 2] if ny > 1 else []) + near + [0]
    for number, hops in enumerate(order):
        t = y_ring.at(hops)
        piece(t, 1 - my_c)
        to_sibling(number, t).start()
        piece(t, my_c)
        to_sibling(number, t).wait_recv()
        pc[t, my_c] = pc[t, my_c] + sib[number]
        if number == 0 and ny > 1:
            y_ring.first()
        elif hops == 1:
            y_ring.early(0)
        elif hops == -1:
            y_ring.early(1)

    share = crops // (nx * nz)
    for px in range(nx):
        lines = slice(px * nz * share, (px + 1) * nz * share)
        cot = jnp.dot(differ[lines, :], pro_t[...], preferred_element_type=F32)
        for pz in range(nz):
            h1[px, pz] = cot[pz * share : (pz + 1) * share, :128]
            h2[pz, px] = cot[pz * share : (pz + 1) * share, 128:]

    zh, xh, sh = max(nz // 2, 1), max(nx // 2, 1), share // 2
    x1 = Ring(
        nx,
        my_x,
        lambda t, half: h1.at[t, pl.ds(half * zh, zh)],
        x1recv,
        x1_sems.at[0],
        x1_sems.at[1],
        on_x,
    )
    z1 = Ring(
        nz,
        my_z,
        lambda t, half: h1.at[my_x, t, pl.ds(half * sh, sh)],
        z1recv,
        z1_sems.at[0],
        z1_sems.at[1],
        on_z,
    )
    z2 = Ring(
        nz,
        my_z,
        lambda t, half: h2.at[t, pl.ds(half * xh, xh)],
        z2recv,
        z2_sems.at[0],
        z2_sems.at[1],
        on_z,
    )
    x2 = Ring(
        nx,
        my_x,
        lambda t, half: h2.at[my_z, t, pl.ds(half * sh, sh)],
        x2recv,
        x2_sems.at[0],
        x2_sems.at[1],
        on_x,
    )
    for ring in (x1, z2):
        ring.first()
        ring.early(0)
        ring.early(1)
    y_ring.second()
    x1.second()
    z2.second()
    loss_x.start(loss_dp.finish())
    z2.step(3)
    x1.finish()
    z1.first()
    z1.early(0)
    z1.early(1)
    z2.step(4)
    z1.second()
    z1.step(3)
    loss_z.start(loss_x.finish())
    y_ring.finish()

    half = depth // 2
    block = aligned(my_dp, width)
    values = pro[:, block].astype(F32)
    inv = inv_norm(jnp.sum(values * values, axis=0, keepdims=True))
    cots = [pc[my_y, my_c, 0], pc[my_y, my_c, 1]]
    along = jnp.sum(cots[0] * values[:half, :], axis=0, keepdims=True) + jnp.sum(
        cots[1] * values[half:, :], axis=0, keepdims=True
    )
    factor = PROTOS / math.sqrt(total_crops)
    pull = along * (inv * inv * inv) * factor
    scale = inv * factor
    ag[my_y, my_c, 0] = cots[0] * scale - values[:half, :] * pull
    ag[my_y, my_c, 1] = cots[1] * scale - values[half:, :] * pull
    y_gather = Gather(
        ny,
        my_y,
        lambda t, part: ag.at[t, my_c, part],
        yg_sems.at[0],
        yg_sems.at[1],
        on_y,
    )
    y_gather.first()

    def share_copy(number, t, core):
        return pltpu.make_async_remote_copy(
            src_ref=ag.at[t, core],
            dst_ref=ag.at[t, core],
            send_sem=sg_sems.at[0, number],
            recv_sem=sg_sems.at[1, number],
            device_id=sibling,
            device_id_type=MESH,
        )

    def out_copy(number, t, core):
        return pltpu.make_async_copy(
            ag.at[t, core],
            out_p.at[:, :, aligned(t * CORES + core, width)],
            op_sems.at[core_slot(core), number],
        )

    def core_slot(core):
        return lax.rem(core + my_c, CORES)

    share_order = [0] + [-h for h in near] + ([ny // 2] if ny > 1 else [])

    def hand_on(number):
        t = y_ring.at(share_order[number])
        share_copy(number, t, my_c).start()
        out_copy(number, t, my_c).start()

    hand_on(0)

    z2.finish()
    x2.first()
    x2.early(0)
    x2.early(1)
    z1.step(4)
    x2.second()
    z1.finish()
    x2.finish()
    mine = pl.ds(pl.multiple_of((my_x * nz + my_z) * share, share), share)
    values = emb[mine, :].astype(F32)
    inv = inv_norm(jnp.sum(values * values, axis=1, keepdims=True))
    cots = [h1[my_x, my_z], h2[my_z, my_x]]
    along = jnp.sum(cots[0] * values[:, :128] + cots[1] * values[:, 128:], axis=1, keepdims=True)
    factor = math.sqrt(PROTOS)
    pull = along * (inv * inv * inv) * factor
    scale = inv * factor
    e1[my_x, my_z] = cots[0] * scale - values[:, :128] * pull
    e2[my_z, my_x] = cots[1] * scale - values[:, 128:] * pull
    z1g = Gather(
        nz,
        my_z,
        lambda t, part: e1.at[my_x, t, pl.ds(part * sh, sh)],
        z1g_sems.at[0],
        z1g_sems.at[1],
        on_z,
    )
    x1g = Gather(
        nx,
        my_x,
        lambda t, part: e1.at[t, pl.ds(part * zh, zh)],
        x1g_sems.at[0],
        x1g_sems.at[1],
        on_x,
    )
    x2g = Gather(
        nx,
        my_x,
        lambda t, part: e2.at[my_z, t, pl.ds(part * sh, sh)],
        x2g_sems.at[0],
        x2g_sems.at[1],
        on_x,
    )
    z2g = Gather(
        nz,
        my_z,
        lambda t, part: e2.at[t, pl.ds(part * xh, xh)],
        z2g_sems.at[0],
        z2g_sems.at[1],
        on_z,
    )
    z1g.first()
    x2g.first()
    if ny >= 4:
        y_gather.take(0, 1)
        hand_on(1)
        y_gather.take(1, 1)
        hand_on(2)
    x2g.rest()
    z2g.first()
    z1g.rest()
    x1g.first()
    out_e1 = []

    def write_e1(px):
        return pltpu.make_async_copy(
            e1.at[px], out_e.at[px, :, :, pl.ds(0, 128)], oe_sems.at[0, px]
        )

    def write_e2(pz):
        return pltpu.make_async_copy(
            e2.at[pz], out_e.at[:, pz, :, pl.ds(128, 128)], oe_sems.at[1, pz]
        )

    z2g.take(0, 1)
    z2g.take(1, 1)
    x1g.take(0, 1)
    x1g.take(1, 1)
    z2g.take(0, 2)
    z2g.take(1, 2)
    if ny > 1:
        y_gather.take(0, ny // 2)
        y_gather.take(1, ny // 2)
        hand_on(len(share_order) - 1)
    for hops in range(2, x1g.far + 1):
        x1g.take(0, hops)
        x1g.take(1, hops)
    for px in range(nx):
        write_e1(px).start()
    for hops in range(3, z2g.far + 1):
        z2g.take(0, hops)
        z2g.take(1, hops)
    for pz in range(nz):
        write_e2(pz).start()
    for number in range(len(share_order)):
        t = y_ring.at(share_order[number])
        share_copy(number, t, 1 - my_c).wait_recv()
        out_copy(number, t, 1 - my_c).start()

    out_l[0, 0] = jnp.sum(loss_z.finish()) / total_crops

    for ring in (y_ring, x1, z1, z2, x2, y_gather, z1g, x1g, x2g, z2g):
        ring.close()
    for number, hops in enumerate(order):
        to_sibling(number, y_ring.at(hops)).wait_send()
    for number in range(len(share_order)):
        t = y_ring.at(share_order[number])
        share_copy(number, t, my_c).wait_send()
        out_copy(number, t, my_c).wait()
        out_copy(number, t, 1 - my_c).wait()
    for px in range(nx):
        write_e1(px).wait()
    for pz in range(nz):
        write_e2(pz).wait()


def local(sizes, embeddings, queue, prototypes, pairing):
    ny, nx, nz = sizes
    dp_count = ny * CORES
    crops, depth = embeddings.shape
    rows = crops + queue.shape[0]
    cols = prototypes.shape[1]
    width = cols // dp_count
    share = crops // (nx * nz)
    row_blocks, crop_blocks, lane_blocks = rows // 128, crops // 128, cols // 128
    half = depth // 2
    fy, fx, fz = max(ny // 2, 1), max(nx // 2, 1), max(nz // 2, 1)
    tile = 256
    dma = pltpu.SemaphoreType.DMA
    vmem = pltpu.VMEM
    scratch = [
        vmem((rows, cols), F32),
        vmem((crops, cols), F32),
        vmem((crops, cols), F32),
        vmem((rows, depth), BF16),
        vmem((crops, depth), BF16),
        vmem((depth, cols), BF16),
        vmem((depth, crops), BF16),
        vmem((cols, depth), BF16),
        vmem((crops, cols), BF16),
        vmem((cols // tile, 8, tile), F32),
        vmem((rows, 128), F32),
        vmem((crops, 128), F32),
        vmem((rows, 128), F32),
        vmem((crops, 128), F32),
        vmem((crops, 128), F32),
        vmem((ITERS, dp_count, lane_blocks, 128), F32),
        vmem((ITERS, nx, row_blocks + crop_blocks, 128), F32),
        vmem((ITERS, nz, row_blocks + crop_blocks, 128), F32),
        vmem((dp_count, 8, 128), F32),
        vmem((nx, 8, 128), F32),
        vmem((nz, 8, 128), F32),
        vmem((ny, CORES, 2, half, width), F32),
        vmem((ny, 2, half, width), F32),
        vmem((2, fy, 2, half, width), F32),
        vmem((ny, CORES, 2, half, width), F32),
        vmem((nx, nz, share, 128), F32),
        vmem((nz, nx, share, 128), F32),
        vmem((2, fx, 2, fz, share, 128), F32),
        vmem((2, fz, 2, share // 2, 128), F32),
        vmem((2, fz, 2, fx, share, 128), F32),
        vmem((2, fx, 2, share // 2, 128), F32),
        vmem((nx, nz, share, 128), F32),
        vmem((nz, nx, share, 128), F32),
        dma((ITERS, 2, dp_count)),
        dma((ITERS, 2, nx)),
        dma((ITERS, 2, nz)),
        dma((2, dp_count)),
        dma((2, nx)),
        dma((2, nz)),
        dma((2, ny)),
        dma((2, 2, fy, 2)),
        dma((2, 2, fx, 2)),
        dma((2, 2, fz, 2)),
        dma((2, 2, fz, 2)),
        dma((2, 2, fx, 2)),
        dma((2, 2, fy, 2)),
        dma((2, ny)),
        dma((2, 2, fz, 2)),
        dma((2, 2, fx, 2)),
        dma((2, 2, fx, 2)),
        dma((2, 2, fz, 2)),
        dma((CORES, ny)),
        dma((2, max(nx, nz))),
    ]
    in_vmem = pl.BlockSpec(memory_space=pltpu.VMEM)
    anywhere = pl.BlockSpec(memory_space=pl.ANY)
    grad_embed, grad_proto, loss = pl.pallas_call(
        functools.partial(kernel, sizes),
        out_shape=(
            jax.ShapeDtypeStruct((nx, nz, share, depth), F32),
            jax.ShapeDtypeStruct((2, half, cols), F32),
            jax.ShapeDtypeStruct((1, 1), F32),
        ),
        in_specs=[in_vmem] * 4,
        out_specs=(anywhere, anywhere, pl.BlockSpec(memory_space=pltpu.SMEM)),
        scratch_shapes=scratch,
        compiler_params=pltpu.CompilerParams(
            collective_id=0, has_side_effects=True, vmem_limit_bytes=60 * 1024 * 1024
        ),
    )(embeddings, queue, prototypes, pairing.reshape(1, crops))
    return (
        grad_embed.reshape(crops, depth),
        grad_proto.reshape(depth, cols),
        loss.reshape(()),
    )


def solution(mesh):
    nx = ALONG_X
    sizes = (mesh.shape["dp"] // CORES, nx, mesh.shape["proto"] // nx)
    return jax.shard_map(
        functools.partial(local, sizes),
        mesh=mesh,
        in_specs=(P("dp", None), P("dp", None), P(None, "proto"), P("dp")),
        out_specs=(P("dp", None), P(None, "proto"), P()),
        check_vma=False,
    )
```

time: 756 us -> 131 us (0.17); the launches traced: 747 us -> 131 us
  blocking collectives: 347 us -> 0 us
  waiting for transfers between devices: 193 us -> 0 us
  Pallas kernels: 0 us -> 124 us
  matrix products: 115 us -> 0 us
  local copies, waits for them, and re-layouts: 45.6 us -> 3.73 us
  other arithmetic: 29.8 us -> 0 us
  between operations: 16.5 us -> 2.47 us
    psum x8 -> x0, blocking collectives: 347 us -> none  [the longest x3 220 us: local(): row_scale = 1.0 / (total_rows * lax.psum(partial_rows, 'proto'))]
    psum x2 -> x0, waiting for transfers between devices: 193 us -> none  [the longest x1 122 us: local(): lax.psum(lax.dot_general(differ, proto_bf, (((1,), (1,)), ((), ())), pref...]
    pallas_call x0 -> x1, Pallas kernels: none -> 124 us  [local(): pl.pallas_call(functools.partial(kernel, sizes), out_shape=(jax.ShapeDtyp...]
    dot_general x9 -> x0, matrix products: 115 us -> none  [the longest x3 52.3 us: local(): jnp.dot(row_scale, exponent, precision=HIGHEST_PREC)]
    gather x3 -> x0, local copies, waits for them, and re-layouts: 26.3 us -> none  [the longest x2 21.7 us: local(): partner_exp = jnp.take(exponent[:crop_rows], local_pair, axis=0)]
    slice x2 -> x0, local copies, waits for them, and re-layouts: 17.4 us -> none  [local(): partner_exp = jnp.take(exponent[:crop_rows], local_pair, axis=0)]
    reduce_sum x7 -> x0, other arithmetic: 15 us -> none  [the longest x1 7.12 us: local(): jnp.sum(codes * scores_crop, axis=1) / TEMPER]
    convert_element_type x2 -> x0, other arithmetic: 8.8 us -> none  [the longest x1 7.26 us: local(): ((soft_exp / soft_total[:, None] - codes) / TEMPER).astype(jnp.bfloat16)]
  transfers between devices with their start and end apart: 2 -> 0, of which waited for: 2 -> 0; matrix products, arithmetic and copies ran while one was open for 1% -> 0% of each run, Pallas kernels for 0% -> 0%
where the time goes in v1:
time: 131 us
  Pallas kernels  124 us (95%)
  local copies, waits for them, and re-layouts  3.73 us (3%)
  between operations  2.47 us (2%)
    pallas_call x1, Pallas kernels, local(): pl.pallas_call(functools.partial(kernel, sizes), out_shape=(jax.ShapeDtyp...  124 us
    unnamed x4, local copies, waits for them, and re-layouts  3.73 us

profile of v1, /device:TPU:2, one launch (start us, length us, event | category | flops | bytes accessed | tf_op | source)
XLA Modules:
  0.0 130.5 jit_solution(7763330186830816658)
XLA Ops:
  0.6 124.3 %shard_map.67 = (f32[4,8,32,256]{3,2,1,0:T(8,128)}, f32[2,128,2048]{2,1,0:T(8,128)}, f32[1,1]{1,0:T(1,128)}) custom-call(bf16[1024,256]{1,0:T(8,128)(2,1)} %emb.1, bf16[1024,256]{1,0:T(8,128)(2,1)} %que.1, bf16[256,2048]{1,0:T(8,128)(2,1)} %pro.1, s32[1,1024]{1,0:T(1,128)} %bitcast.6), custom_call_target="tpu_custom_call" | custom-call | tf_op jit(solution)/shard_map/pallas_call | solution.py:867
  125.0 0.0 copy-start
  125.0 2.4 %copy.10 = f32[1024,256]{1,0:T(8,128)} copy(f32[1024,256]{1,0:T(8,128)} %bitcast.5) | data formatting | bytes 2097152
  127.4 0.0 copy-done
  127.4 1.3 %copy.11 = f32[256,2048]{1,0:T(8,128)} copy(f32[256,2048]{1,0:T(8,128)S(1)} %bitcast.4) | data formatting | bytes 4194304
Async XLA Ops:
  125.0 2.4 %copy-start = (f32[2,128,2048]{2,1,0:T(8,128)S(1)}, f32[2,128,2048]{2,1,0:T(8,128)}, u32[]{:S(2)}) copy-start(f32[2,128,2048]{2,1,0:T(8,128)} %get-tuple-element.7) | copy-start | bytes 6291460

commit v2 on v0

v2 whole, which is shorter than its diff:
```python
import functools
import math

import jax
import jax.numpy as jnp
from jax import lax
from jax.experimental import pallas as pl
from jax.experimental.pallas import tpu as pltpu
from jax.sharding import PartitionSpec as P

PROTOS = 65536
ITERS = 3
CORES = 2
ALONG_X = 4
LOG2E = math.log2(math.e)
F32 = jnp.float32
BF16 = jnp.bfloat16
MESH = pl.DeviceIdType.MESH


def inv_norm(sum_sq):
    shifted = sum_sq + 1e-06
    guess = lax.rsqrt(shifted)
    return guess * (1.5 - 0.5 * shifted * guess * guess)


def aligned(index, size):
    return pl.ds(pl.multiple_of(index * size, size), size)


def remote(src, dst, send_sem, recv_sem, device):
    return pltpu.make_async_remote_copy(
        src_ref=src,
        dst_ref=dst,
        send_sem=send_sem,
        recv_sem=recv_sem,
        device_id=device,
        device_id_type=MESH,
    )


def arrived(view, sems, device):
    remote(view, view, sems.at[0], sems.at[1], device).wait_recv()


def departed(view, sems, device):
    remote(view, view, sems.at[0], sems.at[1], device).wait_send()


def far_first(size):
    return sorted(range(1, size), key=lambda hop: (-min(hop, size - hop), hop))


class Exchange:
    def __init__(self, buf, sems, me, size, device):
        self.buf, self.sems, self.me, self.size, self.device = buf, sems, me, size, device

    def start(self, block):
        self.buf[self.me] = block
        for hop in far_first(self.size):
            slot = self.buf.at[self.me]
            peer = self.device(lax.rem(self.me + hop, self.size))
            remote(slot, slot, self.sems.at[0], self.sems.at[1], peer).start()

    def finish(self):
        others = self.buf.at[pl.ds(0, self.size - 1)]
        arrived(others, self.sems, self.device(self.me))
        departed(others, self.sems, self.device(self.me))
        total = self.buf[0]
        for slot in range(1, self.size):
            total = total + self.buf[slot]
        return total


class Scatter:
    def __init__(self, n, me, part, recv, sems, device):
        self.n, self.me, self.part, self.recv = n, me, part, recv
        self.sems, self.device = sems, device

    def start(self):
        for hop in far_first(self.n):
            piece = lax.rem(self.me + hop, self.n)
            remote(
                self.part(piece),
                self.recv.at[hop - 1],
                self.sems.at[0],
                self.sems.at[1],
                self.device(piece),
            ).start()

    def finish(self):
        arrived(self.recv, self.sems, self.device(self.me))
        total = self.part(self.me)[...]
        for hop in range(1, self.n):
            total = total + self.recv[hop - 1]
        return total

    def close(self):
        departed(self.recv, self.sems, self.device(self.me))


class Ring:
    def __init__(self, n, me, part, recv, sems, recv_sems, device):
        self.n, self.me, self.part, self.recv = n, me, part, recv
        self.sems, self.recv_sems, self.device = sems, recv_sems, device
        self.far = n // 2

    def at(self, hops):
        return lax.rem(self.me + hops + self.n, self.n)

    def copy(self, way, step, half, piece):
        return remote(
            self.part(piece, half),
            self.recv.at[way, step, half],
            self.sems.at[0],
            self.recv_sems.at[way, step],
            self.device(self.at(1 if way == 0 else -1)),
        )

    def add(self, way, step, half, piece):
        view = self.part(piece, half)
        view[...] = view[...] + self.recv[way, step, half]

    def first(self):
        for way in range(2):
            self.copy(way, 0, way, self.at(self.far)).start()

    def early(self, way):
        if self.far == 2:
            self.copy(way, 1, 1 - way, self.at(1 if way == 0 else -1)).start()

    def second(self):
        if self.far == 2:
            for way in range(2):
                piece = self.at(1 if way == 0 else -1)
                self.copy(way, 0, way, piece).wait_recv()
                self.add(way, 0, way, piece)
                self.copy(way, 1, way, piece).start()

    def finish(self):
        for way in range(2):
            if self.far == 2:
                view = self.recv.at[way, 1]
                remote(
                    view,
                    view,
                    self.sems.at[0],
                    self.recv_sems.at[way, 1],
                    self.device(self.me),
                ).wait_recv()
                self.add(way, 1, 0, self.me)
                self.add(way, 1, 1, self.me)
            else:
                self.copy(way, 0, way, self.me).wait_recv()
                self.add(way, 0, way, self.me)


def kernel(
    sizes,
    emb_hbm,
    que_hbm,
    pro_hbm,
    pair_hbm,
    out_e,
    out_p,
    out_l,
    emb,
    que,
    pro,
    pair,
    ex,
    sx,
    yx,
    rows_bf,
    part_bf,
    pro_bf,
    emb_t,
    pro_t,
    differ,
    colacc,
    lanes,
    softp,
    rbc,
    stb,
    qpart,
    dpbuf,
    xbuf,
    zbuf,
    ldp,
    lx,
    lz,
    pc,
    sib,
    yrecv,
    h1,
    h2,
    x1recv,
    z1recv,
    z2recv,
    x2recv,
    load_sems,
    dp_sems,
    x_sems,
    z_sems,
    loss_sems,
    sib_send,
    sib_recv,
    pair_sems,
    ring_sems,
    yg_recv,
    zg_recv,
    xg_recv,
):
    ny, nx, nz = sizes
    dp_count = ny * CORES
    crops, depth = emb.shape
    rows = crops + que.shape[0]
    cols = pro.shape[1]
    total_rows = rows * dp_count
    total_crops = crops * dp_count
    lane_blocks = cols // 128
    row_blocks = rows // 128
    crop_blocks = crops // 128
    width = cols // dp_count
    tile = 256

    my_dp = lax.axis_index("dp")
    my_proto = lax.axis_index("proto")
    my_y, my_c = my_dp // CORES, lax.rem(my_dp, CORES)
    my_z, my_x = my_proto // nx, lax.rem(my_proto, nx)

    def on_dp(index):
        return (index, my_proto)

    def on_x(index):
        return (my_dp, my_z * nx + index)

    def on_z(index):
        return (my_dp, index * nx + my_x)

    def on_y(index):
        return (index * CORES + my_c, my_proto)

    sibling = (my_y * CORES + 1 - my_c, my_proto)

    barrier = pltpu.get_barrier_semaphore()
    for me, size, device in ((my_z, nz, on_z), (my_x, nx, on_x), (my_dp, dp_count, on_dp)):
        for hop in far_first(size):
            pl.semaphore_signal(
                barrier, inc=1, device_id=device(lax.rem(me + hop, size)), device_id_type=MESH
            )

    loads = [
        pltpu.make_async_copy(source, target, load_sems.at[i])
        for i, (source, target) in enumerate(
            ((emb_hbm, emb), (que_hbm, que), (pro_hbm, pro), (pair_hbm, pair))
        )
    ]
    for load in loads:
        load.start()
    for load in loads:
        load.wait()

    @pl.loop(0, crops // tile)
    def _(i):
        block = aligned(i, tile)
        for source, first in ((emb, 0), (que, crops)):
            values = source[block, :].astype(F32)
            inv = inv_norm(jnp.sum(values * values, axis=1, keepdims=True))
            start = pl.multiple_of(first + i * tile, tile)
            rows_bf[pl.ds(start, tile), :] = (values * inv).astype(BF16)

    @pl.loop(0, cols // tile)
    def _(j):
        block = aligned(j, tile)
        values = pro[:, block].astype(F32)
        inv = inv_norm(jnp.sum(values * values, axis=0, keepdims=True))
        pro_bf[:, block] = (values * inv).astype(BF16)

    softp[...] = jnp.zeros_like(softp)

    @pl.loop(0, cols // tile)
    def _(j):
        block = aligned(j, tile)
        weights = pro_bf[:, block]
        acc = jnp.zeros((8, tile), F32)
        for i in range(rows // tile):
            lines = slice(i * tile, (i + 1) * tile)
            scores = jnp.dot(rows_bf[lines, :], weights, preferred_element_type=F32)
            if i < crops // tile:
                sx[lines, block] = scores
                soft = jnp.exp2(scores * (10.0 * LOG2E))
                folded = soft[:, :128]
                for k in range(1, tile // 128):
                    folded = folded + soft[:, k * 128 : (k + 1) * 128]
                softp[lines, :] += folded
                expo = soft * soft
            else:
                expo = jnp.exp2(scores * (20.0 * LOG2E))
            ex[lines, block] = expo
            acc = acc + jnp.sum(expo.reshape(tile // 8, 8, tile), axis=0)
        colacc[j] = acc

    def dense_cols():
        pieces = []
        for j in range(lane_blocks):
            k, part = j * 128 // tile, (j * 128) % tile
            pieces.append(jnp.sum(colacc[k, :, part : part + 128], axis=0, keepdims=True))
        return jnp.concatenate(pieces, axis=0)

    def dense_rows(source, blocks):
        pieces = []
        for b in range(blocks):
            pieces.append(
                jnp.sum(source[b * 128 : (b + 1) * 128, :].T, axis=0, keepdims=True)
            )
        return jnp.concatenate(pieces, axis=0)

    def spread_rows(target, dense, blocks):
        for b in range(blocks):
            target[b * 128 : (b + 1) * 128, :] = jnp.broadcast_to(
                dense[b : b + 1, :], (128, 128)
            ).T

    def col_pass():
        groups = 4

        def step(i, accs):
            accs = list(accs)
            for g in range(groups):
                lines = pl.ds(pl.multiple_of(i * 8 * groups + 8 * g, 8), 8)
                scale = rbc[lines, :]
                for j in range(lane_blocks):
                    accs[j] = accs[j] + ex[lines, j * 128 : (j + 1) * 128] * scale
            return tuple(accs)

        accs = lax.fori_loop(
            0, rows // (8 * groups), step, (jnp.zeros((8, 128), F32),) * lane_blocks
        )
        return jnp.concatenate([jnp.sum(a, axis=0, keepdims=True) for a in accs], axis=0)

    def spread_cols(dense):
        return [
            jnp.broadcast_to(dense[j : j + 1, :], (8, 128)) for j in range(lane_blocks)
        ]

    def row_pass(scales):
        groups = 4

        @pl.loop(0, rows // (8 * groups))
        def _(i):
            for g in range(groups):
                lines = pl.ds(pl.multiple_of(i * 8 * groups + 8 * g, 8), 8)
                acc = ex[lines, :128] * scales[0]
                for j in range(1, lane_blocks):
                    acc = acc + ex[lines, j * 128 : (j + 1) * 128] * scales[j]
                lanes[lines, :] = acc

    def partner_pass(scales):
        groups = 4

        @pl.loop(0, crops // (8 * groups))
        def _(i):
            for g in range(groups):
                lines = pl.ds(pl.multiple_of(i * 8 * groups + 8 * g, 8), 8)
                acc = jnp.zeros((8, 128), F32)
                for j in range(lane_blocks):
                    block = slice(j * 128, (j + 1) * 128)
                    code = yx[lines, block] * scales[j]
                    yx[lines, block] = code
                    acc = acc + code
                lanes[lines, :] = acc

    def soften(first, last):
        groups = 2

        @pl.loop(first // (8 * groups), last // (8 * groups))
        def _(i):
            for g in range(groups):
                lines = pl.ds(pl.multiple_of(i * 8 * groups + 8 * g, 8), 8)
                scale = stb[lines, :]
                acc = jnp.zeros((8, 128), F32)
                for j in range(lane_blocks):
                    block = slice(j * 128, (j + 1) * 128)
                    score = sx[lines, block]
                    acc = acc + yx[lines, block] * score
                    sx[lines, block] = jnp.exp2(score * (10.0 * LOG2E)) * scale
                qpart[lines, :] = acc

    def pick_partners():
        local_pair = pair[...] - my_dp * crops

        @pl.loop(0, crops // tile)
        def _(i):
            block = aligned(i, tile)
            line = lax.broadcasted_iota(jnp.int32, (tile, crops), 0) + i * tile
            pick = jnp.where(line == local_pair, 1.0, 0.0).astype(BF16)
            part_bf[block, :] = jnp.dot(
                pick, rows_bf[:crops, :], preferred_element_type=F32
            ).astype(BF16)

    def partner_exponents():
        @pl.loop(0, cols // tile)
        def _(j):
            block = aligned(j, tile)
            weights = pro_bf[:, block]
            for i in range(crops // tile):
                lines = slice(i * tile, (i + 1) * tile)
                scores = jnp.dot(part_bf[lines, :], weights, preferred_element_type=F32)
                soft = jnp.exp2(scores * (10.0 * LOG2E))
                yx[lines, block] = soft * soft

    def transposed_rows():
        @pl.loop(0, crops // tile)
        def _(i):
            block = aligned(i, tile)
            emb_t[:, block] = rows_bf[block, :].astype(F32).T.astype(BF16)

    def transposed_cols():
        @pl.loop(0, cols // tile)
        def _(j):
            block = aligned(j, tile)
            pro_t[block, :] = pro_bf[:, block].astype(F32).T.astype(BF16)

    pl.semaphore_wait(barrier, dp_count - 1 + nx - 1 + nz - 1)
    col_dense = dense_cols()
    soft_total = None
    row_sum = None
    for it in range(ITERS):
        over_dp = Exchange(dpbuf.at[it], dp_sems.at[it], my_dp, dp_count, on_dp)
        over_x = Exchange(xbuf.at[it], x_sems.at[it], my_x, nx, on_x)
        over_z = Exchange(zbuf.at[it], z_sems.at[it], my_z, nz, on_z)
        over_dp.start(col_dense)
        extra = jnp.zeros((crop_blocks, 128), F32)
        if it == 0:
            pick_partners()
            extra = dense_rows(softp, crop_blocks)
        elif it == 1:
            spread_rows(stb, 10.0 / soft_total, crop_blocks)
        elif it == 2:
            transposed_cols()
        col_scale = 1.0 / (PROTOS * over_dp.finish())
        if it < ITERS - 1:
            row_pass(spread_cols(col_scale))
            over_x.start(jnp.concatenate([dense_rows(lanes, row_blocks), extra], axis=0))
            if it == 0:
                transposed_rows()
            over_z.start(over_x.finish())
            if it == 0:
                partner_exponents()
            total = over_z.finish()
            if it == 0:
                soft_total = total[row_blocks:, :]
            spread_rows(rbc, 1.0 / (total_rows * total[:row_blocks, :]), row_blocks)
            col_dense = col_pass()
        else:
            partner_pass(spread_cols(10.0 * col_scale))
            filler = jnp.zeros((row_blocks, 128), F32)
            over_x.start(
                jnp.concatenate([dense_rows(lanes, crop_blocks), filler], axis=0)
            )
            soften(0, crops // 2)
            over_z.start(over_x.finish())
            soften(crops // 2, crops)
            row_sum = over_z.finish()[:crop_blocks, :]

    spread_rows(rbc, 10.0 / row_sum, crop_blocks)

    repeat = tile // 128
    for i in range(crops // tile):
        lines = slice(i * tile, (i + 1) * tile)
        scale = jnp.concatenate([rbc[lines, :]] * repeat, axis=1)

        @pl.loop(0, cols // tile)
        def _(j):
            block = aligned(j, tile)
            value = sx[lines, block] - yx[lines, block] * scale
            differ[lines, block] = value.astype(BF16)

    share = crops // (nx * nz)
    first_share = share - share // 4
    x_line = nz * share

    x1 = Ring(
        nx,
        my_x,
        lambda t, half: h1.at[t, pl.ds(half * (nz // 2), nz // 2)],
        x1recv,
        ring_sems.at[0],
        pair_sems.at[0],
        on_x,
    )
    z1 = Scatter(nz, my_z, lambda t: h1.at[my_x, t], z1recv, ring_sems.at[1], on_z)
    z2 = Scatter(nz, my_z, lambda t: h2.at[t], z2recv, ring_sems.at[2], on_z)
    x2 = Scatter(nx, my_x, lambda t: h2.at[my_z, t], x2recv, ring_sems.at[3], on_x)
    for hops in [nx // 2] + ([1, -1] if nx == 4 else []) + [0]:
        t = x1.at(hops)
        lines = aligned(t, x_line)
        cot = jnp.dot(differ[lines, :], pro_t[...], preferred_element_type=F32)
        for pz in range(nz):
            h1[t, pz] = cot[pz * share : pz * share + first_share, :]
            h2[pz, t] = cot[pz * share + first_share : (pz + 1) * share, :]
        if hops == nx // 2:
            x1.first()
        elif hops == 1:
            x1.early(0)
        elif hops == -1:
            x1.early(1)
    z2.start()

    half_depth = depth // 2

    def piece(t, core):
        block = aligned(t * CORES + core, width)
        cot = jnp.dot(emb_t[...], differ[:, block], preferred_element_type=F32)
        pc[t, core, 0] = cot[:half_depth, :]
        pc[t, core, 1] = cot[half_depth:, :]

    def to_sibling(number, t):
        return remote(
            pc.at[t, 1 - my_c], sib.at[number], sib_send.at[0], sib_recv.at[number], sibling
        )

    y_ring = Ring(
        ny,
        my_y,
        lambda t, half: pc.at[t, my_c, half],
        yrecv,
        ring_sems.at[4],
        pair_sems.at[1],
        on_y,
    )
    near = [1, -1] if ny == 4 else []
    order = [ny // 2] + near + [0]
    for number, hops in enumerate(order):
        t = y_ring.at(hops)
        piece(t, 1 - my_c)
        to_sibling(number, t).start()
        piece(t, my_c)
        to_sibling(number, t).wait_recv()
        pc[t, my_c] = pc[t, my_c] + sib[number]
        if hops == ny // 2:
            y_ring.first()
        elif hops == 1:
            y_ring.early(0)
        elif hops == -1:
            y_ring.early(1)

    def add_up(i, acc):
        lines = aligned(i, 8)
        return acc + qpart[lines, :] * rbc[lines, :]

    code_score = lax.fori_loop(0, crops // 8, add_up, jnp.zeros((8, 128), F32))
    log_total = jnp.log(soft_total) * (1.0 / (nx * nz))
    if crop_blocks != 8:
        log_total = jnp.broadcast_to(jnp.sum(log_total, axis=0, keepdims=True), (8, 128)) / 8.0
    loss_dp = Exchange(ldp, loss_sems.at[0], my_dp, dp_count, on_dp)
    loss_x = Exchange(lx, loss_sems.at[1], my_x, nx, on_x)
    loss_z = Exchange(lz, loss_sems.at[2], my_z, nz, on_z)
    loss_dp.start(log_total - code_score)

    x1.second()
    y_ring.second()
    loss_x.start(loss_dp.finish())
    h2[my_z] = z2.finish()
    x2.start()
    x1.finish()
    z1.start()
    loss_z.start(loss_x.finish())
    y_ring.finish()

    def columns(t, core):
        return aligned(t * CORES + core, width)

    block = columns(my_y, my_c)
    values = pro[:, block].astype(F32)
    inv = inv_norm(jnp.sum(values * values, axis=0, keepdims=True))
    cots = [pc[my_y, my_c, 0], pc[my_y, my_c, 1]]
    along = jnp.sum(cots[0] * values[:half_depth, :], axis=0, keepdims=True) + jnp.sum(
        cots[1] * values[half_depth:, :], axis=0, keepdims=True
    )
    factor = PROTOS / math.sqrt(total_crops)
    pull = along * (inv * inv * inv) * factor
    scale = inv * factor
    out_p[0, :, block] = cots[0] * scale - values[:half_depth, :] * pull
    out_p[1, :, block] = cots[1] * scale - values[half_depth:, :] * pull

    def along_y(way, step, half, t):
        view = out_p.at[half, :, columns(t, my_c)]
        peer = on_y(y_ring.at(1 if way == 0 else -1))
        return remote(view, view, ring_sems.at[5, 0], yg_recv.at[way, step, half], peer)

    def hand_on(t):
        view = out_p.at[:, :, columns(t, my_c)]
        remote(view, view, ring_sems.at[6, 0], ring_sems.at[6, 1], sibling).start()

    if ny == 4:
        for part in range(2):
            along_y(0, 0, part, my_y).start()
            along_y(1, 0, 1 - part, my_y).start()
    else:
        along_y(0, 1, 0, my_y).start()
        along_y(1, 1, 1, my_y).start()
    hand_on(my_y)

    def pull_rows(cot, first, count):
        values = emb[aligned(my_x * nz + my_z, share), :].astype(F32)
        values = values[first : first + count, :]
        inv = inv_norm(jnp.sum(values * values, axis=1, keepdims=True))
        along = jnp.sum(cot * values, axis=1, keepdims=True)
        factor = math.sqrt(PROTOS)
        out_e[my_x, my_z, pl.ds(first, count)] = cot * (inv * factor) - values * (
            along * (inv * inv * inv) * factor
        )

    rest = share - first_share
    late = pl.ds(first_share, rest)
    soon = pl.ds(0, first_share)

    pull_rows(x2.finish(), first_share, rest)
    for hop in far_first(nx):
        view = out_e.at[my_x, my_z, late]
        remote(
            view, view, ring_sems.at[7, 0], ring_sems.at[7, 1], on_x(x1.at(hop))
        ).start()
    loss_total = loss_z.finish()

    pull_rows(z1.finish(), 0, first_share)

    def z_at(hops):
        return lax.rem(my_z + hops + nz, nz)

    def near_x(way, rel):
        view = out_e.at[my_x, z_at(rel), soon]
        peer = on_x(x1.at(1 if way == 0 else -1))
        return remote(view, view, ring_sems.at[9, 0], xg_recv.at[way, rel], peer)

    def from_x(way, rel):
        view = out_e.at[x1.at(-1 if way == 0 else 1), z_at(rel), soon]
        peer = on_x(x1.at(1 if way == 0 else -1))
        return remote(view, view, ring_sems.at[10, 0], ring_sems.at[10, 1], peer)

    def over_z_at(rel):
        view = out_e.at[my_x, my_z, soon]
        return remote(view, view, ring_sems.at[8, 0], zg_recv.at[rel], on_z(z_at(rel)))

    for hop in sorted(range(1, nz), key=lambda h: (min(h, nz - h), h)):
        over_z_at(hop).start()
    near_x(0, 0).start()
    near_x(1, 0).start()

    pending = sorted(range(nz), key=lambda h: (min(h, nz - h), h))
    ahead = [r for r in pending if 1 <= r <= nz // 2]

    def receive_z(rel):
        view = out_e.at[my_x, z_at(nz - rel), soon]
        remote(view, view, ring_sems.at[8, 0], zg_recv.at[rel], on_z(my_z)).wait_recv()
        near_x(0, nz - rel).start()
        near_x(1, nz - rel).start()

    def take_y(way):
        t = y_ring.at(-1 if way == 0 else 1)
        for part in (way, 1 - way):
            view = out_p.at[part, :, columns(t, my_c)]
            remote(
                view, view, ring_sems.at[5, 0], yg_recv.at[way, 0, part], on_y(my_y)
            ).wait_recv()
            if part == way:
                along_y(way, 1, part, t).start()
        hand_on(t)

    def send_late():
        arrived(out_e.at[pl.ds(0, nx - 1), 0, late], ring_sems.at[7], on_x(my_x))
        for hop in far_first(nz):
            view = out_e.at[:, my_z, late]
            remote(
                view, view, ring_sems.at[11, 0], ring_sems.at[11, 1], on_z(z_at(hop))
            ).start()

    steps = [lambda r=r: receive_z(r) for r in pending[1:]]
    steps.insert(min(2, len(steps)), send_late)
    if ny == 4:
        steps.insert(min(4, len(steps)), lambda: take_y(0))
        steps.insert(min(5, len(steps)), lambda: take_y(1))
    for step in steps:
        step()
    if nx == 4:
        for rel in pending:
            for way in range(2):
                view = out_e.at[x1.at(-1 if way == 0 else 1), z_at(rel), soon]
                remote(
                    view, view, ring_sems.at[9, 0], xg_recv.at[way, rel], on_x(my_x)
                ).wait_recv()
                if (rel in ahead) == (way == 0):
                    from_x(way, rel).start()
    else:
        for rel in pending:
            for way in range(2):
                view = out_e.at[x1.at(-1 if way == 0 else 1), z_at(rel), soon]
                remote(
                    view, view, ring_sems.at[9, 0], xg_recv.at[way, rel], on_x(my_x)
                ).wait_recv()

    far_y = y_ring.at(ny // 2)
    for way in range(2):
        view = out_p.at[way, :, columns(far_y, my_c)]
        remote(
            view, view, ring_sems.at[5, 0], yg_recv.at[way, 1, way], on_y(my_y)
        ).wait_recv()
    hand_on(far_y)
    out_l[0, 0] = jnp.sum(loss_total) / total_crops

    arrived(out_e.at[:, pl.ds(0, nz - 1), late], ring_sems.at[11], on_z(my_z))
    if nx == 4:
        arrived(out_e.at[0, :, soon], ring_sems.at[10], on_x(my_x))
    own = out_p.at[:, :, pl.ds(0, ny * width)]
    arrived(own, ring_sems.at[6], sibling)
    departed(own, ring_sems.at[6], sibling)
    departed(h1.at[pl.ds(0, nx - 1)], ring_sems.at[0], on_x(my_x))
    for ring in (z1, z2, x2):
        ring.close()
    departed(pc.at[pl.ds(0, ny - 1), 0], ring_sems.at[4], on_y(my_y))
    remote(pc.at[:, 0], pc.at[:, 0], sib_send.at[0], sib_recv.at[0], sibling).wait_send()
    departed(out_p.at[:, :, pl.ds(0, (ny - 1) * width)], ring_sems.at[5], on_y(my_y))
    departed(out_e.at[pl.ds(0, nx - 1), 0, late], ring_sems.at[7], on_x(my_x))
    departed(out_e.at[0, pl.ds(0, nz - 1), soon], ring_sems.at[8], on_z(my_z))
    departed(out_e.at[pl.ds(0, 2), :, soon], ring_sems.at[9], on_x(my_x))
    if nx == 4:
        departed(out_e.at[0, :, soon], ring_sems.at[10], on_x(my_x))
    departed(out_e.at[:, pl.ds(0, nz - 1), late], ring_sems.at[11], on_z(my_z))


def local(sizes, embeddings, queue, prototypes, pairing):
    ny, nx, nz = sizes
    dp_count = ny * CORES
    crops, depth = embeddings.shape
    rows = crops + queue.shape[0]
    cols = prototypes.shape[1]
    width = cols // dp_count
    share = crops // (nx * nz)
    first_share = share - share // 4
    rest = share // 4
    row_blocks, crop_blocks, lane_blocks = rows // 128, crops // 128, cols // 128
    half = depth // 2
    tile = 256
    dma = pltpu.SemaphoreType.DMA
    vmem = pltpu.VMEM
    scratch = [
        vmem((crops, depth), BF16),
        vmem((rows - crops, depth), BF16),
        vmem((depth, cols), BF16),
        vmem((1, crops), jnp.int32),
        vmem((rows, cols), F32),
        vmem((crops, cols), F32),
        vmem((crops, cols), F32),
        vmem((rows, depth), BF16),
        vmem((crops, depth), BF16),
        vmem((depth, cols), BF16),
        vmem((depth, crops), BF16),
        vmem((cols, depth), BF16),
        vmem((crops, cols), BF16),
        vmem((cols // tile, 8, tile), F32),
        vmem((rows, 128), F32),
        vmem((crops, 128), F32),
        vmem((rows, 128), F32),
        vmem((crops, 128), F32),
        vmem((crops, 128), F32),
        vmem((ITERS, dp_count, lane_blocks, 128), F32),
        vmem((ITERS, nx, row_blocks + crop_blocks, 128), F32),
        vmem((ITERS, nz, row_blocks + crop_blocks, 128), F32),
        vmem((dp_count, 8, 128), F32),
        vmem((nx, 8, 128), F32),
        vmem((nz, 8, 128), F32),
        vmem((ny, CORES, 2, half, width), F32),
        vmem((ny, 2, half, width), F32),
        vmem((2, 2, 2, half, width), F32),
        vmem((nx, nz, first_share, depth), F32),
        vmem((nz, nx, rest, depth), F32),
        vmem((2, 2, 2, nz // 2, first_share, depth), F32),
        vmem((nz - 1, first_share, depth), F32),
        vmem((nz - 1, nx, rest, depth), F32),
        vmem((nx - 1, rest, depth), F32),
        dma((4,)),
        dma((ITERS, 2)),
        dma((ITERS, 2)),
        dma((ITERS, 2)),
        dma((3, 2)),
        dma((1,)),
        dma((ny,)),
        dma((2, 2, 2)),
        dma((12, 2)),
        dma((2, 2, 2)),
        dma((nz,)),
        dma((2, nz)),
    ]
    in_vmem = pl.BlockSpec(memory_space=pltpu.VMEM)
    anywhere = pl.BlockSpec(memory_space=pl.ANY)
    grad_embed, grad_proto, loss = pl.pallas_call(
        functools.partial(kernel, sizes),
        out_shape=(
            pltpu.VMEM((nx, nz, share, depth), F32),
            pltpu.VMEM((2, half, cols), F32),
            jax.ShapeDtypeStruct((1, 1), F32),
        ),
        in_specs=[anywhere] * 4,
        out_specs=(in_vmem, in_vmem, pl.BlockSpec(memory_space=pltpu.SMEM)),
        scratch_shapes=scratch,
        compiler_params=pltpu.CompilerParams(
            collective_id=0, has_side_effects=True, vmem_limit_bytes=59 * 1024 * 1024
        ),
    )(embeddings, queue, prototypes, pairing.reshape(1, crops))
    return (
        grad_embed.reshape(crops, depth),
        grad_proto.reshape(depth, cols),
        loss.reshape(()),
    )


def solution(mesh):
    nx = ALONG_X
    sizes = (mesh.shape["dp"] // CORES, nx, mesh.shape["proto"] // nx)
    return jax.shard_map(
        functools.partial(local, sizes),
        mesh=mesh,
        in_specs=(P("dp", None), P("dp", None), P(None, "proto"), P("dp")),
        out_specs=(P("dp", None), P(None, "proto"), P()),
        check_vma=False,
    )
```

time: 756 us -> 104 us (0.14); the launches traced: 747 us -> 103 us
  blocking collectives: 347 us -> 0 us
  waiting for transfers between devices: 193 us -> 0 us
  matrix products: 115 us -> 0 us
  Pallas kernels: 0 us -> 98.7 us
  local copies, waits for them, and re-layouts: 45.6 us -> 2.29 us
  other arithmetic: 29.8 us -> 0 us
  between operations: 16.5 us -> 2.33 us
    psum x8 -> x0, blocking collectives: 347 us -> none  [the longest x3 220 us: local(): row_scale = 1.0 / (total_rows * lax.psum(partial_rows, 'proto'))]
    psum x2 -> x0, waiting for transfers between devices: 193 us -> none  [the longest x1 122 us: local(): lax.psum(lax.dot_general(differ, proto_bf, (((1,), (1,)), ((), ())), pref...]
    dot_general x9 -> x0, matrix products: 115 us -> none  [the longest x3 52.3 us: local(): jnp.dot(row_scale, exponent, precision=HIGHEST_PREC)]
    pallas_call x0 -> x1, Pallas kernels: none -> 98.7 us  [local(): pl.pallas_call(functools.partial(kernel, sizes), out_shape=(pltpu.VMEM((n...]
    gather x3 -> x0, local copies, waits for them, and re-layouts: 26.3 us -> none  [the longest x2 21.7 us: local(): partner_exp = jnp.take(exponent[:crop_rows], local_pair, axis=0)]
    slice x2 -> x0, local copies, waits for them, and re-layouts: 17.4 us -> none  [local(): partner_exp = jnp.take(exponent[:crop_rows], local_pair, axis=0)]
    reduce_sum x7 -> x0, other arithmetic: 15 us -> none  [the longest x1 7.12 us: local(): jnp.sum(codes * scores_crop, axis=1) / TEMPER]
    convert_element_type x2 -> x0, other arithmetic: 8.8 us -> none  [the longest x1 7.26 us: local(): ((soft_exp / soft_total[:, None] - codes) / TEMPER).astype(jnp.bfloat16)]
  transfers between devices with their start and end apart: 2 -> 0, of which waited for: 2 -> 0; matrix products, arithmetic and copies ran while one was open for 1% -> 0% of each run, Pallas kernels for 0% -> 0%
where the time goes in v2:
time: 104 us; the launch traced here: 103 us
  Pallas kernels  98.7 us (95%)
  between operations  2.33 us (2%)
  local copies, waits for them, and re-layouts  2.29 us (2%)
    pallas_call x1, Pallas kernels, local(): pl.pallas_call(functools.partial(kernel, sizes), out_shape=(pltpu.VMEM((n...  98.7 us
    unnamed x2, local copies, waits for them, and re-layouts  2.29 us

profile of v2, /device:TPU:2, one launch (start us, length us, event | category | flops | bytes accessed | tf_op | source)
XLA Modules:
  0.0 103.3 jit_solution(6181593984819860802)
XLA Ops:
  0.6 98.7 %shard_map.67 = (f32[4,8,32,256]{3,2,1,0:T(8,128)S(1)}, f32[2,128,2048]{2,1,0:T(8,128)S(1)}, f32[1,1]{1,0:T(1,128)}) custom-call(bf16[1024,256]{1,0:T(8,128)(2,1)} %emb_hbm.1, bf16[1024,256]{1,0:T(8,128)(2,1)} %que_hbm.1, bf16[256,2048]{1,0:T(8,128)(2,1)} %pro_hbm.1, s32[1,1024]{1,0:T(1,128)} %bitcast.6), custom_call_target="tpu_custom_call" | custom-call | tf_op jit(solution)/shard_map/pallas_call | solution.py:798
  99.3 1.0 copy.10
  100.3 1.3 %copy.11 = f32[256,2048]{1,0:T(8,128)} copy(f32[256,2048]{1,0:T(8,128)S(1)} %bitcast.4) | data formatting | bytes 4194304

commit v3 on v2

--- a/solution.py
+++ b/solution.py
@@ -178,7 +178,7 @@
     pro_t,
     differ,
     colacc,
-    lanes,
+    dense,
     softp,
     rbc,
     stb,
@@ -186,6 +186,8 @@
     dpbuf,
     xbuf,
     zbuf,
+    sxbuf,
+    szbuf,
     ldp,
     lx,
     lz,
@@ -202,14 +204,18 @@
     dp_sems,
     x_sems,
     z_sems,
+    soft_sems,
     loss_sems,
     sib_send,
     sib_recv,
-    pair_sems,
+    y_sems,
+    y_pairs,
     ring_sems,
+    x1_sems,
+    x1_pairs,
+    z1_sems,
     yg_recv,
     zg_recv,
-    xg_recv,
 ):
     ny, nx, nz = sizes
     dp_count = ny * CORES
@@ -258,8 +264,8 @@
     ]
     for load in loads:
         load.start()
-    for load in loads:
-        load.wait()
+    loads[0].wait()
+    loads[1].wait()
 
     @pl.loop(0, crops // tile)
     def _(i):
@@ -269,6 +275,9 @@
             inv = inv_norm(jnp.sum(values * values, axis=1, keepdims=True))
             start = pl.multiple_of(first + i * tile, tile)
             rows_bf[pl.ds(start, tile), :] = (values * inv).astype(BF16)
+
+    loads[2].wait()
+    loads[3].wait()
 
     @pl.loop(0, cols // tile)
     def _(j):
@@ -344,32 +353,39 @@
             jnp.broadcast_to(dense[j : j + 1, :], (8, 128)) for j in range(lane_blocks)
         ]
 
+    def row_sums(target, count, line_sums):
+        pair = 2
+
+        @pl.loop(0, count // (128 * pair))
+        def _(i):
+            for k in range(pair):
+                first = (i * pair + k) * 128
+                accs = [
+                    line_sums(pl.ds(pl.multiple_of(first + 8 * g, 8), 8)) for g in range(16)
+                ]
+                turned = jnp.concatenate(accs, axis=0).T
+                target[pl.ds(i * pair + k, 1), :] = jnp.sum(turned, axis=0, keepdims=True)
+
     def row_pass(scales):
-        groups = 4
-
-        @pl.loop(0, rows // (8 * groups))
-        def _(i):
-            for g in range(groups):
-                lines = pl.ds(pl.multiple_of(i * 8 * groups + 8 * g, 8), 8)
-                acc = ex[lines, :128] * scales[0]
-                for j in range(1, lane_blocks):
-                    acc = acc + ex[lines, j * 128 : (j + 1) * 128] * scales[j]
-                lanes[lines, :] = acc
+        def line_sums(lines):
+            acc = ex[lines, :128] * scales[0]
+            for j in range(1, lane_blocks):
+                acc = acc + ex[lines, j * 128 : (j + 1) * 128] * scales[j]
+            return acc
+
+        row_sums(dense, rows, line_sums)
 
     def partner_pass(scales):
-        groups = 4
-
-        @pl.loop(0, crops // (8 * groups))
-        def _(i):
-            for g in range(groups):
-                lines = pl.ds(pl.multiple_of(i * 8 * groups + 8 * g, 8), 8)
-                acc = jnp.zeros((8, 128), F32)
-                for j in range(lane_blocks):
-                    block = slice(j * 128, (j + 1) * 128)
-                    code = yx[lines, block] * scales[j]
-                    yx[lines, block] = code
-                    acc = acc + code
-                lanes[lines, :] = acc
+        def line_sums(lines):
+            acc = jnp.zeros((8, 128), F32)
+            for j in range(lane_blocks):
+                block = slice(j * 128, (j + 1) * 128)
+                code = yx[lines, block] * scales[j]
+                yx[lines, block] = code
+                acc = acc + code
+            return acc
+
+        row_sums(dense, crops, line_sums)
 
     def soften(first, last):
         groups = 2
@@ -426,125 +442,143 @@
     col_dense = dense_cols()
     soft_total = None
     row_sum = None
+    soft_x = Exchange(sxbuf, soft_sems.at[0], my_x, nx, on_x)
+    soft_z = Exchange(szbuf, soft_sems.at[1], my_z, nz, on_z)
     for it in range(ITERS):
+        blocks = pl.ds(0, row_blocks if it < ITERS - 1 else crop_blocks)
         over_dp = Exchange(dpbuf.at[it], dp_sems.at[it], my_dp, dp_count, on_dp)
-        over_x = Exchange(xbuf.at[it], x_sems.at[it], my_x, nx, on_x)
-        over_z = Exchange(zbuf.at[it], z_sems.at[it], my_z, nz, on_z)
+        over_x = Exchange(xbuf.at[it, :, blocks], x_sems.at[it], my_x, nx, on_x)
+        over_z = Exchange(zbuf.at[it, :, blocks], z_sems.at[it], my_z, nz, on_z)
         over_dp.start(col_dense)
-        extra = jnp.zeros((crop_blocks, 128), F32)
         if it == 0:
             pick_partners()
-            extra = dense_rows(softp, crop_blocks)
+            soft_part = dense_rows(softp, crop_blocks)
         elif it == 1:
+            soft_x.start(soft_part)
+            transposed_cols()
+        else:
+            soft_total = soft_z.finish()
             spread_rows(stb, 10.0 / soft_total, crop_blocks)
-        elif it == 2:
-            transposed_cols()
         col_scale = 1.0 / (PROTOS * over_dp.finish())
         if it < ITERS - 1:
             row_pass(spread_cols(col_scale))
-            over_x.start(jnp.concatenate([dense_rows(lanes, row_blocks), extra], axis=0))
+            over_x.start(dense[...])
             if it == 0:
                 transposed_rows()
+            else:
+                soft_z.start(soft_x.finish())
             over_z.start(over_x.finish())
             if it == 0:
                 partner_exponents()
             total = over_z.finish()
-            if it == 0:
-                soft_total = total[row_blocks:, :]
-            spread_rows(rbc, 1.0 / (total_rows * total[:row_blocks, :]), row_blocks)
+            spread_rows(rbc, 1.0 / (total_rows * total), row_blocks)
             col_dense = col_pass()
         else:
             partner_pass(spread_cols(10.0 * col_scale))
-            filler = jnp.zeros((row_blocks, 128), F32)
-            over_x.start(
-                jnp.concatenate([dense_rows(lanes, crop_blocks), filler], axis=0)
-            )
+            over_x.start(dense[:crop_blocks, :])
             soften(0, crops // 2)
             over_z.start(over_x.finish())
             soften(crops // 2, crops)
-            row_sum = over_z.finish()[:crop_blocks, :]
+            row_sum = over_z.finish()
 
     spread_rows(rbc, 10.0 / row_sum, crop_blocks)
 
+    share = crops // (nx * nz)
+    rest = share // 4
+    groups = 3
+    first_share = groups * rest
+    x_line = nz * share
+
+    def x_ring(g):
+        return Ring(
+            nx,
+            my_x,
+            lambda t, half: h1.at[g, t, pl.ds(half * (nz // 2), nz // 2)],
+            x1recv.at[g],
+            x1_sems.at[g],
+            x1_pairs.at[g],
+            on_x,
+        )
+
+    def z_scatter(g):
+        return Scatter(nz, my_z, lambda t: h1.at[g, my_x, t], z1recv.at[g], z1_sems.at[g], on_z)
+
+    x1 = [x_ring(g) for g in range(groups)]
+    z1 = [z_scatter(g) for g in range(groups)]
+    z2 = Scatter(nz, my_z, lambda t: h2.at[t], z2recv, ring_sems.at[2], on_z)
+    x2 = Scatter(nx, my_x, lambda t: h2.at[my_z, t], x2recv, ring_sems.at[3], on_x)
+
     repeat = tile // 128
-    for i in range(crops // tile):
-        lines = slice(i * tile, (i + 1) * tile)
+    for hops in [nx // 2] + ([1, -1] if nx == 4 else []) + [0]:
+        t = x1[0].at(hops)
+        lines = aligned(t, x_line)
         scale = jnp.concatenate([rbc[lines, :]] * repeat, axis=1)
-
-        @pl.loop(0, cols // tile)
-        def _(j):
-            block = aligned(j, tile)
+        for j in range(cols // tile):
+            block = slice(j * tile, (j + 1) * tile)
             value = sx[lines, block] - yx[lines, block] * scale
             differ[lines, block] = value.astype(BF16)
-
-    share = crops // (nx * nz)
-    first_share = share - share // 4
-    x_line = nz * share
-
-    x1 = Ring(
-        nx,
-        my_x,
-        lambda t, half: h1.at[t, pl.ds(half * (nz // 2), nz // 2)],
-        x1recv,
-        ring_sems.at[0],
-        pair_sems.at[0],
-        on_x,
-    )
-    z1 = Scatter(nz, my_z, lambda t: h1.at[my_x, t], z1recv, ring_sems.at[1], on_z)
-    z2 = Scatter(nz, my_z, lambda t: h2.at[t], z2recv, ring_sems.at[2], on_z)
-    x2 = Scatter(nx, my_x, lambda t: h2.at[my_z, t], x2recv, ring_sems.at[3], on_x)
-    for hops in [nx // 2] + ([1, -1] if nx == 4 else []) + [0]:
-        t = x1.at(hops)
-        lines = aligned(t, x_line)
         cot = jnp.dot(differ[lines, :], pro_t[...], preferred_element_type=F32)
         for pz in range(nz):
-            h1[t, pz] = cot[pz * share : pz * share + first_share, :]
+            for g in range(groups):
+                first = pz * share + g * rest
+                h1[g, t, pz] = cot[first : first + rest, :]
             h2[pz, t] = cot[pz * share + first_share : (pz + 1) * share, :]
-        if hops == nx // 2:
-            x1.first()
-        elif hops == 1:
-            x1.early(0)
-        elif hops == -1:
-            x1.early(1)
+        for ring in x1:
+            if hops == nx // 2:
+                ring.first()
+            elif hops == 1:
+                ring.early(0)
+            elif hops == -1:
+                ring.early(1)
     z2.start()
 
     half_depth = depth // 2
+    parts = 2
+    narrow = width // parts
 
     def piece(t, core):
         block = aligned(t * CORES + core, width)
         cot = jnp.dot(emb_t[...], differ[:, block], preferred_element_type=F32)
-        pc[t, core, 0] = cot[:half_depth, :]
-        pc[t, core, 1] = cot[half_depth:, :]
+        for part in range(parts):
+            across = slice(part * narrow, (part + 1) * narrow)
+            pc[part, t, core, 0] = cot[:half_depth, across]
+            pc[part, t, core, 1] = cot[half_depth:, across]
 
     def to_sibling(number, t):
         return remote(
-            pc.at[t, 1 - my_c], sib.at[number], sib_send.at[0], sib_recv.at[number], sibling
+            pc.at[:, t, 1 - my_c], sib.at[number], sib_send.at[0], sib_recv.at[number], sibling
         )
 
-    y_ring = Ring(
-        ny,
-        my_y,
-        lambda t, half: pc.at[t, my_c, half],
-        yrecv,
-        ring_sems.at[4],
-        pair_sems.at[1],
-        on_y,
-    )
+    def y_ring_of(part):
+        return Ring(
+            ny,
+            my_y,
+            lambda t, half: pc.at[part, t, my_c, half],
+            yrecv.at[part],
+            y_sems.at[part],
+            y_pairs.at[part],
+            on_y,
+        )
+
+    y_rings = [y_ring_of(part) for part in range(parts)]
+    y_at = y_rings[0].at
     near = [1, -1] if ny == 4 else []
     order = [ny // 2] + near + [0]
     for number, hops in enumerate(order):
-        t = y_ring.at(hops)
+        t = y_at(hops)
         piece(t, 1 - my_c)
         to_sibling(number, t).start()
         piece(t, my_c)
         to_sibling(number, t).wait_recv()
-        pc[t, my_c] = pc[t, my_c] + sib[number]
+        for part in range(parts):
+            pc[part, t, my_c] = pc[part, t, my_c] + sib[number, part]
         if hops == ny // 2:
-            y_ring.first()
+            y_rings[0].first()
         elif hops == 1:
-            y_ring.early(0)
+            y_rings[0].early(0)
         elif hops == -1:
-            y_ring.early(1)
+            y_rings[0].early(1)
+    y_rings[1].first()
 
     def add_up(i, acc):
         lines = aligned(i, 8)
@@ -559,49 +593,59 @@
     loss_z = Exchange(lz, loss_sems.at[2], my_z, nz, on_z)
     loss_dp.start(log_total - code_score)
 
-    x1.second()
-    y_ring.second()
-    loss_x.start(loss_dp.finish())
+    for ring in x1:
+        ring.second()
+    y_rings[0].second()
+    y_rings[1].early(0)
+    y_rings[1].early(1)
+    for ring, scatter in zip(x1, z1):
+        ring.finish()
+        scatter.start()
+    y_rings[1].second()
     h2[my_z] = z2.finish()
     x2.start()
-    x1.finish()
-    z1.start()
-    loss_z.start(loss_x.finish())
-    y_ring.finish()
-
-    def columns(t, core):
-        return aligned(t * CORES + core, width)
-
-    block = columns(my_y, my_c)
-    values = pro[:, block].astype(F32)
-    inv = inv_norm(jnp.sum(values * values, axis=0, keepdims=True))
-    cots = [pc[my_y, my_c, 0], pc[my_y, my_c, 1]]
-    along = jnp.sum(cots[0] * values[:half_depth, :], axis=0, keepdims=True) + jnp.sum(
-        cots[1] * values[half_depth:, :], axis=0, keepdims=True
-    )
-    factor = PROTOS / math.sqrt(total_crops)
-    pull = along * (inv * inv * inv) * factor
-    scale = inv * factor
-    out_p[0, :, block] = cots[0] * scale - values[:half_depth, :] * pull
-    out_p[1, :, block] = cots[1] * scale - values[half_depth:, :] * pull
-
-    def along_y(way, step, half, t):
-        view = out_p.at[half, :, columns(t, my_c)]
-        peer = on_y(y_ring.at(1 if way == 0 else -1))
-        return remote(view, view, ring_sems.at[5, 0], yg_recv.at[way, step, half], peer)
-
-    def hand_on(t):
-        view = out_p.at[:, :, columns(t, my_c)]
+    loss_x.start(loss_dp.finish())
+
+    def columns(t, core, part):
+        first = (t * CORES + core) * width + part * narrow
+        return pl.ds(pl.multiple_of(first, narrow), narrow)
+
+    def pull_columns(part):
+        block = columns(my_y, my_c, part)
+        values = pro[:, block].astype(F32)
+        inv = inv_norm(jnp.sum(values * values, axis=0, keepdims=True))
+        cots = [pc[part, my_y, my_c, 0], pc[part, my_y, my_c, 1]]
+        along = jnp.sum(cots[0] * values[:half_depth, :], axis=0, keepdims=True) + jnp.sum(
+            cots[1] * values[half_depth:, :], axis=0, keepdims=True
+        )
+        factor = PROTOS / math.sqrt(total_crops)
+        pull = along * (inv * inv * inv) * factor
+        scale = inv * factor
+        out_p[0, :, block] = cots[0] * scale - values[:half_depth, :] * pull
+        out_p[1, :, block] = cots[1] * scale - values[half_depth:, :] * pull
+
+    def along_y(way, step, half, t, part):
+        view = out_p.at[half, :, columns(t, my_c, part)]
+        peer = on_y(y_at(1 if way == 0 else -1))
+        return remote(view, view, ring_sems.at[5, 0], yg_recv.at[part, way, step, half], peer)
+
+    def hand_on(t, part):
+        view = out_p.at[:, :, columns(t, my_c, part)]
         remote(view, view, ring_sems.at[6, 0], ring_sems.at[6, 1], sibling).start()
 
-    if ny == 4:
-        for part in range(2):
-            along_y(0, 0, part, my_y).start()
-            along_y(1, 0, 1 - part, my_y).start()
-    else:
-        along_y(0, 1, 0, my_y).start()
-        along_y(1, 1, 1, my_y).start()
-    hand_on(my_y)
+    def give_y(part):
+        y_rings[part].finish()
+        pull_columns(part)
+        if ny == 4:
+            for half in range(2):
+                along_y(0, 0, half, my_y, part).start()
+                along_y(1, 0, 1 - half, my_y, part).start()
+        else:
+            along_y(0, 1, 0, my_y, part).start()
+            along_y(1, 1, 1, my_y, part).start()
+        hand_on(my_y, part)
+
+    give_y(0)
 
     def pull_rows(cot, first, count):
         values = emb[aligned(my_x * nz + my_z, share), :].astype(F32)
@@ -613,61 +657,41 @@
             along * (inv * inv * inv) * factor
         )
 
-    rest = share - first_share
     late = pl.ds(first_share, rest)
     soon = pl.ds(0, first_share)
+
+    def z_at(hops):
+        return lax.rem(my_z + hops + nz, nz)
+
+    def over_x_from(rel):
+        view = out_e.at[my_x, z_at(rel), soon]
+        for hop in far_first(nx):
+            remote(
+                view, view, ring_sems.at[9, 0], ring_sems.at[9, 1], on_x(x1[0].at(hop))
+            ).start()
+
+    def over_z_at(rel):
+        view = out_e.at[my_x, my_z, soon]
+        return remote(view, view, ring_sems.at[8, 0], zg_recv.at[rel], on_z(z_at(rel)))
 
     pull_rows(x2.finish(), first_share, rest)
     for hop in far_first(nx):
         view = out_e.at[my_x, my_z, late]
         remote(
-            view, view, ring_sems.at[7, 0], ring_sems.at[7, 1], on_x(x1.at(hop))
+            view, view, ring_sems.at[7, 0], ring_sems.at[7, 1], on_x(x1[0].at(hop))
         ).start()
-    loss_total = loss_z.finish()
-
-    pull_rows(z1.finish(), 0, first_share)
-
-    def z_at(hops):
-        return lax.rem(my_z + hops + nz, nz)
-
-    def near_x(way, rel):
+    pull_rows(jnp.concatenate([scatter.finish() for scatter in z1], axis=0), 0, first_share)
+    for hop in far_first(nz):
+        over_z_at(hop).start()
+    over_x_from(0)
+    give_y(1)
+
+    loss_z.start(loss_x.finish())
+
+    def receive_z(rel):
         view = out_e.at[my_x, z_at(rel), soon]
-        peer = on_x(x1.at(1 if way == 0 else -1))
-        return remote(view, view, ring_sems.at[9, 0], xg_recv.at[way, rel], peer)
-
-    def from_x(way, rel):
-        view = out_e.at[x1.at(-1 if way == 0 else 1), z_at(rel), soon]
-        peer = on_x(x1.at(1 if way == 0 else -1))
-        return remote(view, view, ring_sems.at[10, 0], ring_sems.at[10, 1], peer)
-
-    def over_z_at(rel):
-        view = out_e.at[my_x, my_z, soon]
-        return remote(view, view, ring_sems.at[8, 0], zg_recv.at[rel], on_z(z_at(rel)))
-
-    for hop in sorted(range(1, nz), key=lambda h: (min(h, nz - h), h)):
-        over_z_at(hop).start()
-    near_x(0, 0).start()
-    near_x(1, 0).start()
-
-    pending = sorted(range(nz), key=lambda h: (min(h, nz - h), h))
-    ahead = [r for r in pending if 1 <= r <= nz // 2]
-
-    def receive_z(rel):
-        view = out_e.at[my_x, z_at(nz - rel), soon]
-        remote(view, view, ring_sems.at[8, 0], zg_recv.at[rel], on_z(my_z)).wait_recv()
-        near_x(0, nz - rel).start()
-        near_x(1, nz - rel).start()
-
-    def take_y(way):
-        t = y_ring.at(-1 if way == 0 else 1)
-        for part in (way, 1 - way):
-            view = out_p.at[part, :, columns(t, my_c)]
-            remote(
-                view, view, ring_sems.at[5, 0], yg_recv.at[way, 0, part], on_y(my_y)
-            ).wait_recv()
-            if part == way:
-                along_y(way, 1, part, t).start()
-        hand_on(t)
+        remote(view, view, ring_sems.at[8, 0], zg_recv.at[nz - rel], on_z(my_z)).wait_recv()
+        over_x_from(rel)
 
     def send_late():
         arrived(out_e.at[pl.ds(0, nx - 1), 0, late], ring_sems.at[7], on_x(my_x))
@@ -677,56 +701,56 @@
                 view, view, ring_sems.at[11, 0], ring_sems.at[11, 1], on_z(z_at(hop))
             ).start()
 
-    steps = [lambda r=r: receive_z(r) for r in pending[1:]]
-    steps.insert(min(2, len(steps)), send_late)
-    if ny == 4:
-        steps.insert(min(4, len(steps)), lambda: take_y(0))
-        steps.insert(min(5, len(steps)), lambda: take_y(1))
-    for step in steps:
-        step()
-    if nx == 4:
-        for rel in pending:
+    def receive_y(way, step, half, part):
+        t = y_at((-1 if way == 0 else 1) if step == 0 else ny // 2)
+        view = out_p.at[half, :, columns(t, my_c, part)]
+        remote(
+            view, view, ring_sems.at[5, 0], yg_recv.at[part, way, step, half], on_y(my_y)
+        ).wait_recv()
+
+    def near_y(part, first):
+        if ny == 4:
             for way in range(2):
-                view = out_e.at[x1.at(-1 if way == 0 else 1), z_at(rel), soon]
-                remote(
-                    view, view, ring_sems.at[9, 0], xg_recv.at[way, rel], on_x(my_x)
-                ).wait_recv()
-                if (rel in ahead) == (way == 0):
-                    from_x(way, rel).start()
-    else:
-        for rel in pending:
-            for way in range(2):
-                view = out_e.at[x1.at(-1 if way == 0 else 1), z_at(rel), soon]
-                remote(
-                    view, view, ring_sems.at[9, 0], xg_recv.at[way, rel], on_x(my_x)
-                ).wait_recv()
-
-    far_y = y_ring.at(ny // 2)
-    for way in range(2):
-        view = out_p.at[way, :, columns(far_y, my_c)]
-        remote(
-            view, view, ring_sems.at[5, 0], yg_recv.at[way, 1, way], on_y(my_y)
-        ).wait_recv()
-    hand_on(far_y)
-    out_l[0, 0] = jnp.sum(loss_total) / total_crops
+                half = way if first else 1 - way
+                t = y_at(-1 if way == 0 else 1)
+                receive_y(way, 0, half, part)
+                if first:
+                    along_y(way, 1, half, t, part).start()
+                else:
+                    hand_on(t, part)
+
+    pending = [nz - hop for hop in far_first(nz)]
+    near_y(0, True)
+    send_late()
+    for rel in pending[: len(pending) // 2]:
+        receive_z(rel)
+    near_y(1, True)
+    for rel in pending[len(pending) // 2 :]:
+        receive_z(rel)
+    near_y(0, False)
+    near_y(1, False)
+    for part in range(parts):
+        for way in range(2):
+            receive_y(way, 1, way, part)
+        hand_on(y_at(ny // 2), part)
+    out_l[0, 0] = jnp.sum(loss_z.finish()) / total_crops
 
     arrived(out_e.at[:, pl.ds(0, nz - 1), late], ring_sems.at[11], on_z(my_z))
-    if nx == 4:
-        arrived(out_e.at[0, :, soon], ring_sems.at[10], on_x(my_x))
+    arrived(out_e.at[pl.ds(0, nx - 1), :, soon], ring_sems.at[9], on_x(my_x))
     own = out_p.at[:, :, pl.ds(0, ny * width)]
     arrived(own, ring_sems.at[6], sibling)
     departed(own, ring_sems.at[6], sibling)
-    departed(h1.at[pl.ds(0, nx - 1)], ring_sems.at[0], on_x(my_x))
-    for ring in (z1, z2, x2):
+    for g in range(groups):
+        departed(h1.at[g, pl.ds(0, nx - 1)], x1_sems.at[g], on_x(my_x))
+    for ring in (*z1, z2, x2):
         ring.close()
-    departed(pc.at[pl.ds(0, ny - 1), 0], ring_sems.at[4], on_y(my_y))
-    remote(pc.at[:, 0], pc.at[:, 0], sib_send.at[0], sib_recv.at[0], sibling).wait_send()
+    for part in range(parts):
+        departed(pc.at[part, pl.ds(0, ny - 1), 0], y_sems.at[part], on_y(my_y))
+    remote(pc.at[:, :, 0], pc.at[:, :, 0], sib_send.at[0], sib_recv.at[0], sibling).wait_send()
     departed(out_p.at[:, :, pl.ds(0, (ny - 1) * width)], ring_sems.at[5], on_y(my_y))
     departed(out_e.at[pl.ds(0, nx - 1), 0, late], ring_sems.at[7], on_x(my_x))
     departed(out_e.at[0, pl.ds(0, nz - 1), soon], ring_sems.at[8], on_z(my_z))
-    departed(out_e.at[pl.ds(0, 2), :, soon], ring_sems.at[9], on_x(my_x))
-    if nx == 4:
-        departed(out_e.at[0, :, soon], ring_sems.at[10], on_x(my_x))
+    departed(out_e.at[pl.ds(0, nx - 1), :, soon], ring_sems.at[9], on_x(my_x))
     departed(out_e.at[:, pl.ds(0, nz - 1), late], ring_sems.at[11], on_z(my_z))
 
 
@@ -738,7 +762,6 @@
     cols = prototypes.shape[1]
     width = cols // dp_count
     share = crops // (nx * nz)
-    first_share = share - share // 4
     rest = share // 4
     row_blocks, crop_blocks, lane_blocks = rows // 128, crops // 128, cols // 128
     half = depth // 2
@@ -760,38 +783,44 @@
         vmem((cols, depth), BF16),
         vmem((crops, cols), BF16),
         vmem((cols // tile, 8, tile), F32),
-        vmem((rows, 128), F32),
+        vmem((row_blocks, 128), F32),
         vmem((crops, 128), F32),
         vmem((rows, 128), F32),
         vmem((crops, 128), F32),
         vmem((crops, 128), F32),
         vmem((ITERS, dp_count, lane_blocks, 128), F32),
-        vmem((ITERS, nx, row_blocks + crop_blocks, 128), F32),
-        vmem((ITERS, nz, row_blocks + crop_blocks, 128), F32),
+        vmem((ITERS, nx, row_blocks, 128), F32),
+        vmem((ITERS, nz, row_blocks, 128), F32),
+        vmem((nx, crop_blocks, 128), F32),
+        vmem((nz, crop_blocks, 128), F32),
         vmem((dp_count, 8, 128), F32),
         vmem((nx, 8, 128), F32),
         vmem((nz, 8, 128), F32),
-        vmem((ny, CORES, 2, half, width), F32),
-        vmem((ny, 2, half, width), F32),
-        vmem((2, 2, 2, half, width), F32),
-        vmem((nx, nz, first_share, depth), F32),
+        vmem((2, ny, CORES, 2, half, width // 2), F32),
+        vmem((ny, 2, 2, half, width // 2), F32),
+        vmem((2, 2, 2, 2, half, width // 2), F32),
+        vmem((3, nx, nz, rest, depth), F32),
         vmem((nz, nx, rest, depth), F32),
-        vmem((2, 2, 2, nz // 2, first_share, depth), F32),
-        vmem((nz - 1, first_share, depth), F32),
+        vmem((3, 2, 2, 2, nz // 2, rest, depth), F32),
+        vmem((3, nz - 1, rest, depth), F32),
         vmem((nz - 1, nx, rest, depth), F32),
         vmem((nx - 1, rest, depth), F32),
         dma((4,)),
         dma((ITERS, 2)),
         dma((ITERS, 2)),
         dma((ITERS, 2)),
+        dma((2, 2)),
         dma((3, 2)),
         dma((1,)),
         dma((ny,)),
+        dma((2, 2)),
         dma((2, 2, 2)),
         dma((12, 2)),
-        dma((2, 2, 2)),
+        dma((3, 2)),
+        dma((3, 2, 2)),
+        dma((3, 2)),
+        dma((2, 2, 2, 2)),
         dma((nz,)),
-        dma((2, nz)),
     ]
     in_vmem = pl.BlockSpec(memory_space=pltpu.VMEM)
     anywhere = pl.BlockSpec(memory_space=pl.ANY)

time: 104 us -> 97.5 us (0.938)
  Pallas kernels: 98.7 us -> 92.6 us
    pallas_call x1, Pallas kernels: 98.7 us -> 92.6 us  [local(): pl.pallas_call(functools.partial(kernel, sizes), out_shape=(pltpu.VMEM((n...]
where the time goes in v3:
time: 97.5 us; the launch traced here: 97.3 us
  Pallas kernels  92.6 us (95%)
  between operations  2.33 us (2%)
  local copies, waits for them, and re-layouts  2.29 us (2%)
    pallas_call x1, Pallas kernels, local(): pl.pallas_call(functools.partial(kernel, sizes), out_shape=(pltpu.VMEM((n...  92.6 us
    unnamed x2, local copies, waits for them, and re-layouts  2.29 us

profile of v3, /device:TPU:2, one launch (start us, length us, event | category | flops | bytes accessed | tf_op | source)
XLA Modules:
  0.0 97.3 jit_solution(2854993903009784767)
XLA Ops:
  0.6 92.6 %shard_map.67 = (f32[4,8,32,256]{3,2,1,0:T(8,128)S(1)}, f32[2,128,2048]{2,1,0:T(8,128)S(1)}, f32[1,1]{1,0:T(1,128)}) custom-call(bf16[1024,256]{1,0:T(8,128)(2,1)} %emb_hbm.1, bf16[1024,256]{1,0:T(8,128)(2,1)} %que_hbm.1, bf16[256,2048]{1,0:T(8,128)(2,1)} %pro_hbm.1, s32[1,1024]{1,0:T(1,128)} %bitcast.6), custom_call_target="tpu_custom_call" | custom-call | tf_op jit(solution)/shard_map/pallas_call | solution.py:827
  93.3 1.0 %copy.10 = f32[1024,256]{1,0:T(8,128)} copy(f32[1024,256]{1,0:T(8,128)S(1)} %bitcast.5) | data formatting | bytes 2097152
  94.2 1.3 %copy.11 = f32[256,2048]{1,0:T(8,128)} copy(f32[256,2048]{1,0:T(8,128)S(1)} %bitcast.4) | data formatting | bytes 4194304

commit v4 on v3

--- a/solution.py
+++ b/solution.py
@@ -249,13 +249,6 @@
 
     sibling = (my_y * CORES + 1 - my_c, my_proto)
 
-    barrier = pltpu.get_barrier_semaphore()
-    for me, size, device in ((my_z, nz, on_z), (my_x, nx, on_x), (my_dp, dp_count, on_dp)):
-        for hop in far_first(size):
-            pl.semaphore_signal(
-                barrier, inc=1, device_id=device(lax.rem(me + hop, size)), device_id_type=MESH
-            )
-
     loads = [
         pltpu.make_async_copy(source, target, load_sems.at[i])
         for i, (source, target) in enumerate(
@@ -264,6 +257,13 @@
     ]
     for load in loads:
         load.start()
+    barrier = pltpu.get_barrier_semaphore()
+    for me, size, device in ((my_z, nz, on_z), (my_x, nx, on_x), (my_dp, dp_count, on_dp)):
+        for hop in far_first(size):
+            pl.semaphore_signal(
+                barrier, inc=1, device_id=device(lax.rem(me + hop, size)), device_id_type=MESH
+            )
+
     loads[0].wait()
     loads[1].wait()
 
@@ -325,13 +325,13 @@
             )
         return jnp.concatenate(pieces, axis=0)
 
-    def spread_rows(target, dense, blocks):
+    def spread_rows(target, dense, blocks, first=0):
         for b in range(blocks):
-            target[b * 128 : (b + 1) * 128, :] = jnp.broadcast_to(
+            target[(first + b) * 128 : (first + b + 1) * 128, :] = jnp.broadcast_to(
                 dense[b : b + 1, :], (128, 128)
             ).T
 
-    def col_pass():
+    def col_pass(first, last, accs):
         groups = 4
 
         def step(i, accs):
@@ -343,20 +343,17 @@
                     accs[j] = accs[j] + ex[lines, j * 128 : (j + 1) * 128] * scale
             return tuple(accs)
 
-        accs = lax.fori_loop(
-            0, rows // (8 * groups), step, (jnp.zeros((8, 128), F32),) * lane_blocks
-        )
-        return jnp.concatenate([jnp.sum(a, axis=0, keepdims=True) for a in accs], axis=0)
+        return lax.fori_loop(first // (8 * groups), last // (8 * groups), step, accs)
 
     def spread_cols(dense):
         return [
             jnp.broadcast_to(dense[j : j + 1, :], (8, 128)) for j in range(lane_blocks)
         ]
 
-    def row_sums(target, count, line_sums):
+    def row_sums(target, start, count, line_sums):
         pair = 2
 
-        @pl.loop(0, count // (128 * pair))
+        @pl.loop(start // (128 * pair), (start + count) // (128 * pair))
         def _(i):
             for k in range(pair):
                 first = (i * pair + k) * 128
@@ -366,14 +363,14 @@
                 turned = jnp.concatenate(accs, axis=0).T
                 target[pl.ds(i * pair + k, 1), :] = jnp.sum(turned, axis=0, keepdims=True)
 
-    def row_pass(scales):
+    def row_pass(scales, start, count):
         def line_sums(lines):
             acc = ex[lines, :128] * scales[0]
             for j in range(1, lane_blocks):
                 acc = acc + ex[lines, j * 128 : (j + 1) * 128] * scales[j]
             return acc
 
-        row_sums(dense, rows, line_sums)
+        row_sums(dense, start, count, line_sums)
 
     def partner_pass(scales):
         def line_sums(lines):
@@ -385,7 +382,7 @@
                 acc = acc + code
             return acc
 
-        row_sums(dense, crops, line_sums)
+        row_sums(dense, 0, crops, line_sums)
 
     def soften(first, last):
         groups = 2
@@ -444,11 +441,29 @@
     row_sum = None
     soft_x = Exchange(sxbuf, soft_sems.at[0], my_x, nx, on_x)
     soft_z = Exchange(szbuf, soft_sems.at[1], my_z, nz, on_z)
+    half_blocks = row_blocks // 2
     for it in range(ITERS):
-        blocks = pl.ds(0, row_blocks if it < ITERS - 1 else crop_blocks)
         over_dp = Exchange(dpbuf.at[it], dp_sems.at[it], my_dp, dp_count, on_dp)
-        over_x = Exchange(xbuf.at[it, :, blocks], x_sems.at[it], my_x, nx, on_x)
-        over_z = Exchange(zbuf.at[it, :, blocks], z_sems.at[it], my_z, nz, on_z)
+        over_x = [
+            Exchange(
+                xbuf.at[it, :, pl.ds(h * half_blocks, half_blocks)],
+                x_sems.at[it, h],
+                my_x,
+                nx,
+                on_x,
+            )
+            for h in range(2)
+        ]
+        over_z = [
+            Exchange(
+                zbuf.at[it, :, pl.ds(h * half_blocks, half_blocks)],
+                z_sems.at[it, h],
+                my_z,
+                nz,
+                on_z,
+            )
+            for h in range(2)
+        ]
         over_dp.start(col_dense)
         if it == 0:
             pick_partners()
@@ -461,25 +476,33 @@
             spread_rows(stb, 10.0 / soft_total, crop_blocks)
         col_scale = 1.0 / (PROTOS * over_dp.finish())
         if it < ITERS - 1:
-            row_pass(spread_cols(col_scale))
-            over_x.start(dense[...])
+            scales = spread_cols(col_scale)
+            for h in range(2):
+                row_pass(scales, h * (rows // 2), rows // 2)
+                over_x[h].start(dense[h * half_blocks : (h + 1) * half_blocks, :])
             if it == 0:
                 transposed_rows()
             else:
                 soft_z.start(soft_x.finish())
-            over_z.start(over_x.finish())
+            for h in range(2):
+                over_z[h].start(over_x[h].finish())
             if it == 0:
                 partner_exponents()
-            total = over_z.finish()
-            spread_rows(rbc, 1.0 / (total_rows * total), row_blocks)
-            col_dense = col_pass()
+            accs = (jnp.zeros((8, 128), F32),) * lane_blocks
+            for h in range(2):
+                scale = 1.0 / (total_rows * over_z[h].finish())
+                spread_rows(rbc, scale, half_blocks, h * half_blocks)
+                accs = col_pass(h * (rows // 2), (h + 1) * (rows // 2), accs)
+            col_dense = jnp.concatenate(
+                [jnp.sum(a, axis=0, keepdims=True) for a in accs], axis=0
+            )
         else:
             partner_pass(spread_cols(10.0 * col_scale))
-            over_x.start(dense[:crop_blocks, :])
+            over_x[0].start(dense[:crop_blocks, :])
             soften(0, crops // 2)
-            over_z.start(over_x.finish())
+            over_z[0].start(over_x[0].finish())
             soften(crops // 2, crops)
-            row_sum = over_z.finish()
+            row_sum = over_z[0].finish()
 
     spread_rows(rbc, 10.0 / row_sum, crop_blocks)
 
@@ -601,7 +624,8 @@
     for ring, scatter in zip(x1, z1):
         ring.finish()
         scatter.start()
-    y_rings[1].second()
+        if ring is x1[0]:
+            y_rings[1].second()
     h2[my_z] = z2.finish()
     x2.start()
     loss_x.start(loss_dp.finish())
@@ -680,11 +704,11 @@
         remote(
             view, view, ring_sems.at[7, 0], ring_sems.at[7, 1], on_x(x1[0].at(hop))
         ).start()
+    give_y(1)
     pull_rows(jnp.concatenate([scatter.finish() for scatter in z1], axis=0), 0, first_share)
     for hop in far_first(nz):
         over_z_at(hop).start()
     over_x_from(0)
-    give_y(1)
 
     loss_z.start(loss_x.finish())
 
@@ -721,11 +745,9 @@
 
     pending = [nz - hop for hop in far_first(nz)]
     near_y(0, True)
+    near_y(1, True)
     send_late()
-    for rel in pending[: len(pending) // 2]:
-        receive_z(rel)
-    near_y(1, True)
-    for rel in pending[len(pending) // 2 :]:
+    for rel in pending:
         receive_z(rel)
     near_y(0, False)
     near_y(1, False)
@@ -807,8 +829,8 @@
         vmem((nx - 1, rest, depth), F32),
         dma((4,)),
         dma((ITERS, 2)),
-        dma((ITERS, 2)),
-        dma((ITERS, 2)),
+        dma((ITERS, 2, 2)),
+        dma((ITERS, 2, 2)),
         dma((2, 2)),
         dma((3, 2)),
         dma((1,)),

time: 97.5 us -> 95.8 us (0.983)
  Pallas kernels: 92.6 us -> 91 us
    pallas_call x1, Pallas kernels: 92.6 us -> 91 us  [local(): pl.pallas_call(functools.partial(kernel, sizes), out_shape=(pltpu.VMEM((n...]
where the time goes in v4:
time: 95.8 us; the launch traced here: 95.7 us
  Pallas kernels  91 us (95%)
  between operations  2.33 us (2%)
  local copies, waits for them, and re-layouts  2.29 us (2%)
    pallas_call x1, Pallas kernels, local(): pl.pallas_call(functools.partial(kernel, sizes), out_shape=(pltpu.VMEM((n...  91 us
    unnamed x2, local copies, waits for them, and re-layouts  2.29 us

profile of v4, /device:TPU:2, one launch (start us, length us, event | category | flops | bytes accessed | tf_op | source)
XLA Modules:
  0.0 95.7 jit_solution(4866512708383985669)
XLA Ops:
  0.6 91.0 %shard_map.67 = (f32[4,8,32,256]{3,2,1,0:T(8,128)S(1)}, f32[2,128,2048]{2,1,0:T(8,128)S(1)}, f32[1,1]{1,0:T(1,128)}) custom-call(bf16[1024,256]{1,0:T(8,128)(2,1)} %emb_hbm.1, bf16[1024,256]{1,0:T(8,128)(2,1)} %que_hbm.1, bf16[256,2048]{1,0:T(8,128)(2,1)} %pro_hbm.1, s32[1,1024]{1,0:T(1,128)} %bitcast.6), custom_call_target="tpu_custom_call" | custom-call | tf_op jit(solution)/shard_map/pallas_call | solution.py:849
  91.7 1.0 %copy.10 = f32[1024,256]{1,0:T(8,128)} copy(f32[1024,256]{1,0:T(8,128)S(1)} %bitcast.5) | data formatting | bytes 2097152
  92.7 1.3 %copy.11 = f32[256,2048]{1,0:T(8,128)} copy(f32[256,2048]{1,0:T(8,128)S(1)} %bitcast.4) | data formatting | bytes 4194304

commit v5 on v4

--- a/solution.py
+++ b/solution.py
@@ -286,13 +286,14 @@
         inv = inv_norm(jnp.sum(values * values, axis=0, keepdims=True))
         pro_bf[:, block] = (values * inv).astype(BF16)
 
+    wide = colacc.shape[2]
     softp[...] = jnp.zeros_like(softp)
 
-    @pl.loop(0, cols // tile)
+    @pl.loop(0, cols // wide)
     def _(j):
-        block = aligned(j, tile)
+        block = aligned(j, wide)
         weights = pro_bf[:, block]
-        acc = jnp.zeros((8, tile), F32)
+        acc = jnp.zeros((8, wide), F32)
         for i in range(rows // tile):
             lines = slice(i * tile, (i + 1) * tile)
             scores = jnp.dot(rows_bf[lines, :], weights, preferred_element_type=F32)
@@ -300,20 +301,20 @@
                 sx[lines, block] = scores
                 soft = jnp.exp2(scores * (10.0 * LOG2E))
                 folded = soft[:, :128]
-                for k in range(1, tile // 128):
+                for k in range(1, wide // 128):
                     folded = folded + soft[:, k * 128 : (k + 1) * 128]
                 softp[lines, :] += folded
                 expo = soft * soft
             else:
                 expo = jnp.exp2(scores * (20.0 * LOG2E))
             ex[lines, block] = expo
-            acc = acc + jnp.sum(expo.reshape(tile // 8, 8, tile), axis=0)
+            acc = acc + jnp.sum(expo.reshape(tile // 8, 8, wide), axis=0)
         colacc[j] = acc
 
     def dense_cols():
         pieces = []
         for j in range(lane_blocks):
-            k, part = j * 128 // tile, (j * 128) % tile
+            k, part = j * 128 // wide, (j * 128) % wide
             pieces.append(jnp.sum(colacc[k, :, part : part + 128], axis=0, keepdims=True))
         return jnp.concatenate(pieces, axis=0)
 
@@ -628,7 +629,6 @@
             y_rings[1].second()
     h2[my_z] = z2.finish()
     x2.start()
-    loss_x.start(loss_dp.finish())
 
     def columns(t, core, part):
         first = (t * CORES + core) * width + part * narrow
@@ -691,12 +691,12 @@
         view = out_e.at[my_x, z_at(rel), soon]
         for hop in far_first(nx):
             remote(
-                view, view, ring_sems.at[9, 0], ring_sems.at[9, 1], on_x(x1[0].at(hop))
+                view, view, ring_sems.at[1, 0], ring_sems.at[1, 1], on_x(x1[0].at(hop))
             ).start()
 
     def over_z_at(rel):
         view = out_e.at[my_x, my_z, soon]
-        return remote(view, view, ring_sems.at[8, 0], zg_recv.at[rel], on_z(z_at(rel)))
+        return remote(view, view, ring_sems.at[4, 0], zg_recv.at[rel], on_z(z_at(rel)))
 
     pull_rows(x2.finish(), first_share, rest)
     for hop in far_first(nx):
@@ -710,11 +710,11 @@
         over_z_at(hop).start()
     over_x_from(0)
 
-    loss_z.start(loss_x.finish())
+    loss_x.start(loss_dp.finish())
 
     def receive_z(rel):
         view = out_e.at[my_x, z_at(rel), soon]
-        remote(view, view, ring_sems.at[8, 0], zg_recv.at[nz - rel], on_z(my_z)).wait_recv()
+        remote(view, view, ring_sems.at[4, 0], zg_recv.at[nz - rel], on_z(my_z)).wait_recv()
         over_x_from(rel)
 
     def send_late():
@@ -722,7 +722,7 @@
         for hop in far_first(nz):
             view = out_e.at[:, my_z, late]
             remote(
-                view, view, ring_sems.at[11, 0], ring_sems.at[11, 1], on_z(z_at(hop))
+                view, view, ring_sems.at[0, 0], ring_sems.at[0, 1], on_z(z_at(hop))
             ).start()
 
     def receive_y(way, step, half, part):
@@ -750,6 +750,7 @@
     for rel in pending:
         receive_z(rel)
     near_y(0, False)
+    loss_z.start(loss_x.finish())
     near_y(1, False)
     for part in range(parts):
         for way in range(2):
@@ -757,8 +758,8 @@
         hand_on(y_at(ny // 2), part)
     out_l[0, 0] = jnp.sum(loss_z.finish()) / total_crops
 
-    arrived(out_e.at[:, pl.ds(0, nz - 1), late], ring_sems.at[11], on_z(my_z))
-    arrived(out_e.at[pl.ds(0, nx - 1), :, soon], ring_sems.at[9], on_x(my_x))
+    arrived(out_e.at[:, pl.ds(0, nz - 1), late], ring_sems.at[0], on_z(my_z))
+    arrived(out_e.at[pl.ds(0, nx - 1), :, soon], ring_sems.at[1], on_x(my_x))
     own = out_p.at[:, :, pl.ds(0, ny * width)]
     arrived(own, ring_sems.at[6], sibling)
     departed(own, ring_sems.at[6], sibling)
@@ -771,9 +772,9 @@
     remote(pc.at[:, :, 0], pc.at[:, :, 0], sib_send.at[0], sib_recv.at[0], sibling).wait_send()
     departed(out_p.at[:, :, pl.ds(0, (ny - 1) * width)], ring_sems.at[5], on_y(my_y))
     departed(out_e.at[pl.ds(0, nx - 1), 0, late], ring_sems.at[7], on_x(my_x))
-    departed(out_e.at[0, pl.ds(0, nz - 1), soon], ring_sems.at[8], on_z(my_z))
-    departed(out_e.at[pl.ds(0, nx - 1), :, soon], ring_sems.at[9], on_x(my_x))
-    departed(out_e.at[:, pl.ds(0, nz - 1), late], ring_sems.at[11], on_z(my_z))
+    departed(out_e.at[0, pl.ds(0, nz - 1), soon], ring_sems.at[4], on_z(my_z))
+    departed(out_e.at[pl.ds(0, nx - 1), :, soon], ring_sems.at[1], on_x(my_x))
+    departed(out_e.at[:, pl.ds(0, nz - 1), late], ring_sems.at[0], on_z(my_z))
 
 
 def local(sizes, embeddings, queue, prototypes, pairing):
@@ -804,7 +805,7 @@
         vmem((depth, crops), BF16),
         vmem((cols, depth), BF16),
         vmem((crops, cols), BF16),
-        vmem((cols // tile, 8, tile), F32),
+        vmem((cols // 512, 8, 512), F32),
         vmem((row_blocks, 128), F32),
         vmem((crops, 128), F32),
         vmem((rows, 128), F32),
@@ -837,7 +838,7 @@
         dma((ny,)),
         dma((2, 2)),
         dma((2, 2, 2)),
-        dma((12, 2)),
+        dma((8, 2)),
         dma((3, 2)),
         dma((3, 2, 2)),
         dma((3, 2)),

time: 95.8 us -> 94.2 us (0.983)
  Pallas kernels: 91 us -> 89.5 us
    pallas_call x1, Pallas kernels: 91 us -> 89.5 us  [local(): pl.pallas_call(functools.partial(kernel, sizes), out_shape=(pltpu.VMEM((n...]
where the time goes in v5:
time: 94.2 us; the launch traced here: 94.1 us
  Pallas kernels  89.5 us (95%)
  between operations  2.33 us (2%)
  local copies, waits for them, and re-layouts  2.29 us (2%)
    pallas_call x1, Pallas kernels, local(): pl.pallas_call(functools.partial(kernel, sizes), out_shape=(pltpu.VMEM((n...  89.5 us
    unnamed x2, local copies, waits for them, and re-layouts  2.29 us

profile of v5, /device:TPU:2, one launch (start us, length us, event | category | flops | bytes accessed | tf_op | source)
XLA Modules:
  0.0 94.1 jit_solution(823534718013072480)
XLA Ops:
  0.6 89.5 %shard_map.67 = (f32[4,8,32,256]{3,2,1,0:T(8,128)S(1)}, f32[2,128,2048]{2,1,0:T(8,128)S(1)}, f32[1,1]{1,0:T(1,128)}) custom-call(bf16[1024,256]{1,0:T(8,128)(2,1)} %emb_hbm.1, bf16[1024,256]{1,0:T(8,128)(2,1)} %que_hbm.1, bf16[256,2048]{1,0:T(8,128)(2,1)} %pro_hbm.1, s32[1,1024]{1,0:T(1,128)} %bitcast.6), custom_call_target="tpu_custom_call" | custom-call | tf_op jit(solution)/shard_map/pallas_call | solution.py:850
  90.1 1.0 %copy.10 = f32[1024,256]{1,0:T(8,128)} copy(f32[1024,256]{1,0:T(8,128)S(1)} %bitcast.5) | data formatting | bytes 2097152
  91.1 1.3 %copy.11 = f32[256,2048]{1,0:T(8,128)} copy(f32[256,2048]{1,0:T(8,128)S(1)} %bitcast.4) | data formatting | bytes 4194304

commit v6 on v5

--- a/solution.py
+++ b/solution.py
@@ -805,7 +805,7 @@
         vmem((depth, crops), BF16),
         vmem((cols, depth), BF16),
         vmem((crops, cols), BF16),
-        vmem((cols // 512, 8, 512), F32),
+        vmem((cols // 1024, 8, 1024), F32),
         vmem((row_blocks, 128), F32),
         vmem((crops, 128), F32),
         vmem((rows, 128), F32),

time: 94.2 us -> 94 us (level)
  no operation moved by 1% of the time
where the time goes in v6:
time: 94 us; the launch traced here: 93.9 us
  Pallas kernels  89.3 us (95%)
  between operations  2.33 us (2%)
  local copies, waits for them, and re-layouts  2.29 us (2%)
    pallas_call x1, Pallas kernels, local(): pl.pallas_call(functools.partial(kernel, sizes), out_shape=(pltpu.VMEM((n...  89.3 us
    unnamed x2, local copies, waits for them, and re-layouts  2.29 us

profile of v6, /device:TPU:2, one launch (start us, length us, event | category | flops | bytes accessed | tf_op | source)
XLA Modules:
  0.0 93.9 jit_solution(11239262041147911062)
XLA Ops:
  0.6 89.3 %shard_map.67 = (f32[4,8,32,256]{3,2,1,0:T(8,128)S(1)}, f32[2,128,2048]{2,1,0:T(8,128)S(1)}, f32[1,1]{1,0:T(1,128)}) custom-call(bf16[1024,256]{1,0:T(8,128)(2,1)} %emb_hbm.1, bf16[1024,256]{1,0:T(8,128)(2,1)} %que_hbm.1, bf16[256,2048]{1,0:T(8,128)(2,1)} %pro_hbm.1, s32[1,1024]{1,0:T(1,128)} %bitcast.6), custom_call_target="tpu_custom_call" | custom-call | tf_op jit(solution)/shard_map/pallas_call | solution.py:850
  89.9 1.0 %copy.10 = f32[1024,256]{1,0:T(8,128)} copy(f32[1024,256]{1,0:T(8,128)S(1)} %bitcast.5) | data formatting | bytes 2097152
  90.9 1.3 %copy.11 = f32[256,2048]{1,0:T(8,128)} copy(f32[256,2048]{1,0:T(8,128)S(1)} %bitcast.4) | data formatting | bytes 4194304
